TPU v7x, 128 devices: a whole 4x4x4 slice. The times are simulated.
128 devices in a mesh: shot: 8 (over x, y_hi), slab: 16 (over y_lo, z, core).
Axes of the slice: x: 4, y: 4 (y_hi: 2, y_lo: 2; y = y_hi * 2 + y_lo), z: 4, core: 2. Of those that a mesh axis runs over, the one named last changes fastest.
Arguments:
- velocity: bfloat16 [192, 128, 256], P('shot', 'slab'), may hold values from 0.099609375 to 0.29882812
- epsilon: bfloat16 [192, 128, 256], P('shot', 'slab'), may hold values from 0.19921875 to 0.3984375
- delta: bfloat16 [192, 128, 256], P('shot', 'slab'), may hold values from 0 to 0.19921875
- tilt: bfloat16 [192, 128, 256], P('shot', 'slab'), may hold values from -3.140625 to 3.140625
- azimuth: bfloat16 [192, 128, 256], P('shot', 'slab'), may hold values from -3.140625 to 3.140625
- offsets: int32 [8, 2], replicated, may hold values from 0 to 128, as said below
- sources: int32 [8], P('shot'), may hold values from 0 to 1572863
- traces: float32 [8, 12], P('shot'), may hold values from -60 to 60
- adjoint_state: float32 [4, 8, 192, 64, 128], P(None, 'shot', 'slab'), may hold values from -6 to 6
- snapshots: bfloat16 [12, 2, 8, 192, 64, 128], P(None, None, 'shot', 'slab'), may hold values from -1.1953125 to 1.1953125
Outputs:
- gradients: float32 [5, 192, 128, 256], P(None, 'shot', 'slab')
- adjoint_final: float32 [2, 8, 192, 64, 128], P(None, 'shot', 'slab')
Inputs may be any that keep to these rules, and one draw needn't show every extreme that they name: offsets[s] = (first lateral, second lateral) earth cell of the aperture's first cell; the first is at most 64, the second at most 128. sources[s] names the cell z * 64 * 128 + x * 128 + y of shot s's aperture.
All inputs are finite; a program needn't handle non-finite values.
Results may differ from a plain program's by a relative error of at most 0.0008.
Values may be sent and summed in bfloat16 or wider, within the bound.
A program may use at most 192 MiB of HBM per device.

v0:
```python
import jax
import jax.numpy as jnp
from jax import lax
from jax.sharding import PartitionSpec as P

centred_second = (-205.0 / 72.0, 8.0 / 5.0, -1.0 / 5.0, 8.0 / 315.0, -1.0 / 560.0)
centred_first = (4.0 / 5.0, -1.0 / 5.0, 4.0 / 105.0, -1.0 / 280.0)


def padded_2(x, sides, width):
    for axis, dim in sides:
        size, length = (lax.axis_size(axis), x.shape[dim])
        up = [(i, (i + 1) % size) for i in range(size - 1)]
        down = [(j, i) for i, j in up]
        last = lax.slice_in_dim(x, length - width, length, axis=dim)
        first = lax.slice_in_dim(x, 0, width, axis=dim)
        before = lax.ppermute(last, axis, up)
        after = lax.ppermute(first, axis, down)
        x = jnp.concatenate([before, x, after], axis=dim)
    return x


def shifted(source_field, along_axis, distance):
    length = source_field.shape[along_axis]
    widths = [(0, 0)] * source_field.ndim
    widths[along_axis] = (4, 4)
    padded = jnp.pad(source_field, widths)
    return lax.slice_in_dim(padded, 4 + distance, 4 + distance + length, axis=along_axis)


def second_along(source_field, along_axis):
    summed = centred_second[0] * source_field
    for distance in range(1, 5):
        summed = summed + centred_second[distance] * (
            shifted(source_field, along_axis, distance)
            + shifted(source_field, along_axis, -distance)
        )
    return summed


def first_along(source_field, along_axis):
    summed = centred_first[0] * (
        shifted(source_field, along_axis, 1) - shifted(source_field, along_axis, -1)
    )
    for distance in range(2, 5):
        summed = summed + centred_first[distance - 1] * (
            shifted(source_field, along_axis, distance)
            - shifted(source_field, along_axis, -distance)
        )
    return summed


def rows_second(extended, row_count):
    summed = centred_second[0] * extended[4 : 4 + row_count]
    for distance in range(1, 5):
        summed = summed + centred_second[distance] * (
            extended[4 + distance : 4 + distance + row_count]
            + extended[4 - distance : 4 - distance + row_count]
        )
    return summed


def rows_first(extended, row_count):
    summed = centred_first[0] * (extended[5 : 5 + row_count] - extended[3 : 3 + row_count])
    for distance in range(2, 5):
        summed = summed + centred_first[distance - 1] * (
            extended[4 + distance : 4 + distance + row_count]
            - extended[4 - distance : 4 - distance + row_count]
        )
    return summed


def derivatives(extended):
    row_count = extended.shape[0] - 8
    centre = extended[4 : 4 + row_count]
    along_x = first_along(extended, 1)
    along_y = first_along(extended, 2)
    return (
        rows_second(extended, row_count),
        second_along(centre, 1),
        second_along(centre, 2),
        rows_first(along_x, row_count),
        rows_first(along_y, row_count),
        first_along(along_x[4 : 4 + row_count], 2),
    )


def quadratic(first_vector, second_vector, second_parts):
    summed = (
        first_vector[0] * second_vector[0] * second_parts[0]
        + first_vector[1] * second_vector[1] * second_parts[1]
    )
    summed = summed + first_vector[2] * second_vector[2] * second_parts[2]
    summed = (
        summed
        + (first_vector[0] * second_vector[1] + first_vector[1] * second_vector[0])
        * second_parts[3]
    )
    summed = (
        summed
        + (first_vector[0] * second_vector[2] + first_vector[2] * second_vector[0])
        * second_parts[4]
    )
    return (
        summed
        + (first_vector[1] * second_vector[2] + first_vector[2] * second_vector[1])
        * second_parts[5]
    )


def prepare(parameters):
    wavespeed = parameters[0]
    tilt_sine = jnp.sin(parameters[3])
    tilt_cosine = jnp.cos(parameters[3])
    azimuth_sine = jnp.sin(parameters[4])
    azimuth_cosine = jnp.cos(parameters[4])
    normal = (tilt_cosine, tilt_sine * azimuth_cosine, tilt_sine * azimuth_sine)
    tilted = (-tilt_sine, tilt_cosine * azimuth_cosine, tilt_cosine * azimuth_sine)
    turned = (jnp.zeros_like(wavespeed), -tilt_sine * azimuth_sine, tilt_sine * azimuth_cosine)
    return (
        (
            wavespeed,
            wavespeed * wavespeed,
            1.0 + 2.0 * parameters[1],
            jnp.sqrt(1.0 + 2.0 * parameters[2]),
        )
        + normal
        + tilted
        + turned
    )


def advance(
    primary_ext,
    coupled_ext,
    primary_prev,
    coupled_prev,
    prepared,
    first_row,
    total_rows,
    amplitude,
    source,
):
    factor = prepared[1]
    stretch = prepared[2]
    coupling = prepared[3]
    normal = prepared[4:7]
    tilted = prepared[7:10]
    turned = prepared[10:13]
    row_count = primary_prev.shape[0]
    across = primary_prev.shape[1]
    lane_count = primary_prev.shape[2]
    parts_primary = derivatives(primary_ext)
    parts_coupled = derivatives(coupled_ext)
    axial_primary = quadratic(normal, normal, parts_primary)
    across_primary = parts_primary[0] + parts_primary[1] + parts_primary[2] - axial_primary
    axial_coupled = quadratic(normal, normal, parts_coupled)
    drive_primary = stretch * across_primary + coupling * axial_coupled
    drive_coupled = coupling * across_primary + axial_coupled
    tilt_primary = 2.0 * quadratic(tilted, normal, parts_primary)
    tilt_coupled = 2.0 * quadratic(tilted, normal, parts_coupled)
    turn_primary = 2.0 * quadratic(turned, normal, parts_primary)
    turn_coupled = 2.0 * quadratic(turned, normal, parts_coupled)
    depth_index = first_row + lax.broadcasted_iota(jnp.int32, (row_count, 1, 1), 0)
    column_index = lax.broadcasted_iota(jnp.int32, (1, across, 1), 1)
    lane_index = lax.broadcasted_iota(jnp.int32, (1, 1, lane_count), 2)
    source_depth = source // (across * lane_count)
    source_column = source // lane_count % across
    source_lane = source % lane_count
    at_source = (
        (depth_index == source_depth)
        & (column_index == source_column)
        & (lane_index == source_lane)
    )
    inside = (depth_index >= 0) & (depth_index < total_rows)
    centre_primary = primary_ext[4 : 4 + row_count]
    centre_coupled = coupled_ext[4 : 4 + row_count]
    primary_next = (
        2.0 * centre_primary
        - primary_prev
        + factor * drive_primary
        + jnp.where(at_source, factor * amplitude, 0.0)
    )
    coupled_next = 2.0 * centre_coupled - coupled_prev + factor * drive_coupled
    primary_next = jnp.where(inside, primary_next, 0.0)
    coupled_next = jnp.where(inside, coupled_next, 0.0)
    images = (
        drive_primary,
        drive_coupled,
        across_primary,
        axial_coupled,
        tilt_primary,
        tilt_coupled,
        turn_primary,
        turn_coupled,
    )
    return (primary_next, coupled_next, images)


def correlate(gradients, images, prepared, forward_primary, forward_coupled):
    wavespeed = prepared[0]
    factor = prepared[1]
    stretch = prepared[2]
    coupling = prepared[3]
    (
        drive_primary,
        drive_coupled,
        across_primary,
        axial_coupled,
        tilt_primary,
        tilt_coupled,
        turn_primary,
        turn_coupled,
    ) = images
    increments = jnp.stack(
        [
            2.0 * wavespeed * (drive_primary * forward_primary + drive_coupled * forward_coupled),
            2.0 * factor * across_primary * forward_primary,
            factor
            / coupling
            * (axial_coupled * forward_primary + across_primary * forward_coupled),
            factor
            * (
                (coupling * tilt_coupled - stretch * tilt_primary) * forward_primary
                + (tilt_coupled - coupling * tilt_primary) * forward_coupled
            ),
            factor
            * (
                (coupling * turn_coupled - stretch * turn_primary) * forward_primary
                + (turn_coupled - coupling * turn_primary) * forward_coupled
            ),
        ]
    )
    return gradients + increments


def on_device(
    velocity, epsilon, delta, tilt, azimuth, offsets, sources, traces, adjoint_state, snapshots
):
    shot_index = lax.axis_index("shot")
    slab_index = lax.axis_index("slab")
    slab_count = lax.axis_size("slab")
    owned_model = jnp.stack([velocity, epsilon, delta, tilt, azimuth])
    owned_width = owned_model.shape[2]
    model_lanes = owned_model.shape[3]
    row_count = adjoint_state.shape[2]
    across = adjoint_state.shape[3]
    lane_count = adjoint_state.shape[4]
    total_rows = row_count * slab_count
    step_count = snapshots.shape[0]
    column_start = offsets[shot_index, 0]
    lane_start = offsets[shot_index, 1]
    source = sources[0]
    amplitudes = traces[0]
    column = lax.all_gather(owned_model, "shot", axis=1, tiled=True)
    column = lax.dynamic_slice_in_dim(column, lane_start, lane_count, 3)
    pieces = lax.all_to_all(column, "slab", split_axis=1, concat_axis=2, tiled=True)
    model_width = pieces.shape[2]
    aperture = lax.dynamic_slice_in_dim(pieces, column_start, across, 2)
    prepared = prepare(aperture.astype(jnp.float32))
    first_row = slab_index * row_count
    gradient_zero = jnp.zeros((5, row_count, across, lane_count), jnp.float32)
    initial = (
        adjoint_state[0, 0],
        adjoint_state[1, 0],
        adjoint_state[2, 0],
        adjoint_state[3, 0],
        gradient_zero,
    )

    def one_step(step_index, carry):
        primary, coupled, primary_prev, coupled_prev, gradients = carry
        widened = padded_2(jnp.stack([primary, coupled]), (("slab", 1),), 4)
        primary_next, coupled_next, images = advance(
            widened[0],
            widened[1],
            primary_prev,
            coupled_prev,
            prepared,
            first_row,
            total_rows,
            amplitudes[step_index],
            source,
        )
        frame = snapshots[step_index]
        gradients = correlate(
            gradients,
            images,
            prepared,
            frame[0, 0].astype(jnp.float32),
            frame[1, 0].astype(jnp.float32),
        )
        return (primary_next, coupled_next, primary, coupled, gradients)

    final = lax.fori_loop(0, step_count, one_step, initial)
    padded = jnp.zeros((5, row_count, model_width, lane_count), jnp.float32)
    padded = lax.dynamic_update_slice_in_dim(padded, final[4], column_start, 2)
    column_grads = lax.all_to_all(padded, "slab", split_axis=2, concat_axis=1, tiled=True)
    spread = jnp.zeros((5, total_rows, owned_width, model_lanes), jnp.float32)
    spread = lax.dynamic_update_slice_in_dim(spread, column_grads, lane_start, 3)
    owner_grads = lax.psum_scatter(spread, "shot", scatter_dimension=1, tiled=True)
    adjoint_final = jnp.stack([final[0], final[1]])[:, None]
    return (owner_grads, adjoint_final)


def solution(mesh):
    return jax.shard_map(
        on_device,
        mesh=mesh,
        in_specs=(
            P("shot", "slab", None),
            P("shot", "slab", None),
            P("shot", "slab", None),
            P("shot", "slab", None),
            P("shot", "slab", None),
            P(),
            P("shot"),
            P("shot", None),
            P(None, "shot", "slab", None, None),
            P(None, None, "shot", "slab", None, None),
        ),
        out_specs=(P(None, "shot", "slab", None), P(None, "shot", "slab", None, None)),
        check_vma=False,
    )
```

profile of v0, /device:TPU:80, one launch (start us, length us, event | category | flops | bytes accessed | tf_op | source)
XLA Modules:
  0.0 1027.3 jit_solution(7787003843859738293)
XLA Ops:
  15.8 65.2 %all-gather.2.cloned.1.call-done = bf16[5,192,8,256]{3,2,0,1:T(8,128)(2,1)} async-done(((bf16[5,24,8,256]{3,2,0,1:T(8,128)(2,1)}), bf16[5,192,8,256]{3,2,0,1:T(8,128)(2,1)}) %all-gather.2.cloned.1.call-update) | async-done | bytes 3932176 | tf_op jit(solution)/shard_map/all_gather | solution.py:255
  81.0 4.1 constant_dynamic-slice_fusion.1
  85.1 6.3 all-to-all-start
  96.3 19.4 %all-to-all-done = bf16[5,192,8,128]{3,2,0,1:T(8,128)(2,1)} async-done(((bf16[5,192,8,128]{3,2,0,1:T(8,128)(2,1)}), bf16[5,192,8,128]{3,2,0,1:T(8,128)(2,1)}, u32[]{:S(2)}, u32[]{:S(2)}) %all-to-all-start) | async-done | bytes 1966112 | tf_op jit(solution)/shard_map/all_to_all | solution.py:257
  118.2 3.9 multiply_add_fusion.3
  124.4 4.7 fusion.196
  129.1 519.2 %while.27 = (s32[]{:T(128)}, f32[12,64,128]{2,1,0:T(8,128)S(1)}, f32[12,64,128]{2,1,0:T(8,128)S(1)}, f32[12,64,128]{2,1,0:T(8,128)}, f32[12,64,128]{2,1,0:T(8,12...) while((s32[]{:T(128)}, f32[12,64,128]{2,1,0:T(8,128)S(1)}, ...), condition=%wide.region_1.2_spmd.clone, body=%wide.region_0.1_spmd.clone.sunk | while | flops 37684224 | bytes 139398560 | solution.py:295
  146.6 10.5 %fusion.221 = (f32[5,12,64,128]{3,2,1,0:T(8,128)}, f32[12,64,128]{2,1,0:T(8,128)}, f32[12,64,128]{2,1,0:T(8,128)S(1)}, f32[12,64,128]{2,1,0:T(8,128)}, f32[12,64...) fusion(f32[12,64,128]{2,1,0:T(8,128)} %get-tuple-element.1750, ...), kind=kLoop, calls=%fused_computation.166.clone.1 | loop fusion | flops 17399808 | bytes 30670856 | tf_op jit(solution)/shard_map/while
  176.9 4.1 collective-permute-done.1
  187.8 10.4 %fusion.221 = (f32[5,12,64,128]{3,2,1,0:T(8,128)}, f32[12,64,128]{2,1,0:T(8,128)}, f32[12,64,128]{2,1,0:T(8,128)S(1)}, f32[12,64,128]{2,1,0:T(8,128)}, f32[12,64...) fusion(f32[12,64,128]{2,1,0:T(8,128)} %get-tuple-element.1750, ...), kind=kLoop, calls=%fused_computation.166.clone.1 | loop fusion | flops 17399808 | bytes 30670856 | tf_op jit(solution)/shard_map/while
  224.5 3.9 fusion.220
  230.2 10.4 %fusion.221 = (f32[5,12,64,128]{3,2,1,0:T(8,128)}, f32[12,64,128]{2,1,0:T(8,128)}, f32[12,64,128]{2,1,0:T(8,128)S(1)}, f32[12,64,128]{2,1,0:T(8,128)}, f32[12,64...) fusion(f32[12,64,128]{2,1,0:T(8,128)} %get-tuple-element.1750, ...), kind=kLoop, calls=%fused_computation.166.clone.1 | loop fusion | flops 17399808 | bytes 30670856 | tf_op jit(solution)/shard_map/while
  272.6 10.4 %fusion.221 = (f32[5,12,64,128]{3,2,1,0:T(8,128)}, f32[12,64,128]{2,1,0:T(8,128)}, f32[12,64,128]{2,1,0:T(8,128)S(1)}, f32[12,64,128]{2,1,0:T(8,128)}, f32[12,64...) fusion(f32[12,64,128]{2,1,0:T(8,128)} %get-tuple-element.1750, ...), kind=kLoop, calls=%fused_computation.166.clone.1 | loop fusion | flops 17399808 | bytes 30670856 | tf_op jit(solution)/shard_map/while
  315.1 10.4 %fusion.221 = (f32[5,12,64,128]{3,2,1,0:T(8,128)}, f32[12,64,128]{2,1,0:T(8,128)}, f32[12,64,128]{2,1,0:T(8,128)S(1)}, f32[12,64,128]{2,1,0:T(8,128)}, f32[12,64...) fusion(f32[12,64,128]{2,1,0:T(8,128)} %get-tuple-element.1750, ...), kind=kLoop, calls=%fused_computation.166.clone.1 | loop fusion | flops 17399808 | bytes 30670856 | tf_op jit(solution)/shard_map/while
  343.1 4.0 collective-permute-start.1
  357.5 10.4 %fusion.221 = (f32[5,12,64,128]{3,2,1,0:T(8,128)}, f32[12,64,128]{2,1,0:T(8,128)}, f32[12,64,128]{2,1,0:T(8,128)S(1)}, f32[12,64,128]{2,1,0:T(8,128)}, f32[12,64...) fusion(f32[12,64,128]{2,1,0:T(8,128)} %get-tuple-element.1750, ...), kind=kLoop, calls=%fused_computation.166.clone.1 | loop fusion | flops 17399808 | bytes 30670856 | tf_op jit(solution)/shard_map/while
  385.5 6.1 collective-permute-start.1
  399.9 10.5 %fusion.221 = (f32[5,12,64,128]{3,2,1,0:T(8,128)}, f32[12,64,128]{2,1,0:T(8,128)}, f32[12,64,128]{2,1,0:T(8,128)S(1)}, f32[12,64,128]{2,1,0:T(8,128)}, f32[12,64...) fusion(f32[12,64,128]{2,1,0:T(8,128)} %get-tuple-element.1750, ...), kind=kLoop, calls=%fused_computation.166.clone.1 | loop fusion | flops 17399808 | bytes 30670856 | tf_op jit(solution)/shard_map/while
  428.0 8.2 collective-permute-start.1
  444.1 10.4 %fusion.221 = (f32[5,12,64,128]{3,2,1,0:T(8,128)}, f32[12,64,128]{2,1,0:T(8,128)}, f32[12,64,128]{2,1,0:T(8,128)S(1)}, f32[12,64,128]{2,1,0:T(8,128)}, f32[12,64...) fusion(f32[12,64,128]{2,1,0:T(8,128)} %get-tuple-element.1750, ...), kind=kLoop, calls=%fused_computation.166.clone.1 | loop fusion | flops 17399808 | bytes 30670856 | tf_op jit(solution)/shard_map/while
  472.1 8.7 collective-permute-start.1
  488.6 10.5 %fusion.221 = (f32[5,12,64,128]{3,2,1,0:T(8,128)}, f32[12,64,128]{2,1,0:T(8,128)}, f32[12,64,128]{2,1,0:T(8,128)S(1)}, f32[12,64,128]{2,1,0:T(8,128)}, f32[12,64...) fusion(f32[12,64,128]{2,1,0:T(8,128)} %get-tuple-element.1750, ...), kind=kLoop, calls=%fused_computation.166.clone.1 | loop fusion | flops 17399808 | bytes 30670856 | tf_op jit(solution)/shard_map/while
  516.6 8.7 collective-permute-start.1
  533.2 10.4 %fusion.221 = (f32[5,12,64,128]{3,2,1,0:T(8,128)}, f32[12,64,128]{2,1,0:T(8,128)}, f32[12,64,128]{2,1,0:T(8,128)S(1)}, f32[12,64,128]{2,1,0:T(8,128)}, f32[12,64...) fusion(f32[12,64,128]{2,1,0:T(8,128)} %get-tuple-element.1750, ...), kind=kLoop, calls=%fused_computation.166.clone.1 | loop fusion | flops 17399808 | bytes 30670856 | tf_op jit(solution)/shard_map/while
  561.1 8.7 collective-permute-start.1
  577.7 10.4 %fusion.221 = (f32[5,12,64,128]{3,2,1,0:T(8,128)}, f32[12,64,128]{2,1,0:T(8,128)}, f32[12,64,128]{2,1,0:T(8,128)S(1)}, f32[12,64,128]{2,1,0:T(8,128)}, f32[12,64...) fusion(f32[12,64,128]{2,1,0:T(8,128)} %get-tuple-element.1750, ...), kind=kLoop, calls=%fused_computation.166.clone.1 | loop fusion | flops 17399808 | bytes 30670856 | tf_op jit(solution)/shard_map/while
  605.7 8.7 collective-permute-start.1
  622.3 10.4 %fusion.221 = (f32[5,12,64,128]{3,2,1,0:T(8,128)}, f32[12,64,128]{2,1,0:T(8,128)}, f32[12,64,128]{2,1,0:T(8,128)S(1)}, f32[12,64,128]{2,1,0:T(8,128)}, f32[12,64...) fusion(f32[12,64,128]{2,1,0:T(8,128)} %get-tuple-element.1750, ...), kind=kLoop, calls=%fused_computation.166.clone.1 | loop fusion | flops 17399808 | bytes 30670856 | tf_op jit(solution)/shard_map/while
  651.6 80.6 %all_to_all.36 = f32[5,12,128,128]{3,1,0,2:T(8,128)S(1)} all-to-all(f32[5,12,128,128]{3,1,0,2:T(8,128)S(1)} %copy_dynamic-update-slice_fusion), channel_id=1, replica_groups=mesh['shot'=8,'slab'=16] {'slab'}, dimensions={2} | all-to-all | bytes 7864320 | tf_op jit(solution)/shard_map/all_to_all | solution.py:298
  739.7 156.9 %dynamic_update_slice.7 = f32[5,192,8,256]{3,2,1,0:T(8,128)} dynamic-update-slice(f32[5,192,8,256]{3,2,1,0:T(8,128)} %broadcast_in_dim.54, f32[5,192,8,128]{3,2,1,0:T(8,128)} %bitcast.283, s32[]{:T(128)} %constant.278.clone.1, s32[]{:T(128)} %constant.278.clone.1, s32[]{:T(128)} %constant.278.clone.1, s32[]{:T(128)S(6)} %select_n.124) | dynamic-update-slice | bytes 7864324 | tf_op jit(solution)/shard_map/dynamic_update_slice | solution.py:300
  900.3 6.1 copy.27
  907.3 110.6 %reduce-scatter.5.cloned.1.call-done = f32[24,10240]{1,0:T(8,128)} async-done(((f32[192,10240]{1,0:T(8,128)}), f32[24,10240]{1,0:T(8,128)}) %reduce-scatter.5.cloned.1.call-update) | async-done | bytes 983056
  (1102 shorter events, 359.0 us)
Async XLA Ops:
  7.2 73.8 %all-gather.2.cloned.1.call-start = ((), (), s32[]{:S(2)}) async-start(), calls=%async_computation.3 | async-start | bytes 4423680 | tf_op jit(solution)/shard_map/all_gather | solution.py:255
  85.1 30.6 %all-to-all-start = ((bf16[5,192,8,128]{3,2,0,1:T(8,128)(2,1)}), bf16[5,192,8,128]{3,2,0,1:T(8,128)(2,1)}, u32[]{:S(2)}, u32[]{:S(2)}) async-start(bf16[5,192,8,128]{3,2,0,1:T(8,128)(2,1)} %constant_dynamic-slice_fusion.1), calls=%async_computation | async-start | bytes 3932160 | tf_op jit(solution)/shard_map/all_to_all | solution.py:257
  91.4 926.5 %reduce-scatter.5.cloned.1.call-start = ((), (), s32[]{:S(2)}) async-start(), calls=%async_computation.4 | async-start | bytes 8847360
  129.2 6.9 collective-permute-start
  132.2 7.7 collective-permute-start.1
  171.1 5.8 collective-permute-start
  173.1 8.0 collective-permute-start.1
  213.8 5.8 collective-permute-start
  215.8 7.7 collective-permute-start.1
  256.3 5.8 collective-permute-start
  258.2 7.7 collective-permute-start.1
  283.1 7.1 copy-start.24
  283.1 7.1 copy-start.25
  283.1 7.1 copy-start.26
  283.1 7.1 copy-start.31
  298.7 5.8 collective-permute-start
  300.6 7.7 collective-permute-start.1
  341.1 6.7 collective-permute-start
  343.1 7.7 collective-permute-start.1
  383.6 8.8 collective-permute-start
  385.5 7.7 collective-permute-start.1
  426.0 10.9 %collective-permute-start = (f32[2,4,64,128]{3,2,1,0:T(8,128)S(1)}, f32[2,4,64,128]{3,2,1,0:T(8,128)S(1)}, u32[]{:S(2)}, u32[]{:S(2)}) collective-permute-start(f32[2,4,64,128]{3,2,1,0:T(8,128)S(1)} %get-tuple-element.1621), channel_id=1, source_target_pairs={{1,0},{2,1},{3,2},{4,3},{5,4},{6,5},{7,6},{8,7},{9,8},{10,9},{11,1... | collective-permute-start | bytes 786440 | tf_op jit(solution)/shard_map/while/body/eval_jaxpr/ppermute | solution.py:18
  428.0 9.4 collective-permute-start.1
  454.5 7.1 copy-start.24
  470.1 11.3 %collective-permute-start = (f32[2,4,64,128]{3,2,1,0:T(8,128)S(1)}, f32[2,4,64,128]{3,2,1,0:T(8,128)S(1)}, u32[]{:S(2)}, u32[]{:S(2)}) collective-permute-start(f32[2,4,64,128]{3,2,1,0:T(8,128)S(1)} %get-tuple-element.1621), channel_id=1, source_target_pairs={{1,0},{2,1},{3,2},{4,3},{5,4},{6,5},{7,6},{8,7},{9,8},{10,9},{11,1... | collective-permute-start | bytes 786440 | tf_op jit(solution)/shard_map/while/body/eval_jaxpr/ppermute | solution.py:18
  472.1 9.8 collective-permute-start.1
  514.7 11.3 %collective-permute-start = (f32[2,4,64,128]{3,2,1,0:T(8,128)S(1)}, f32[2,4,64,128]{3,2,1,0:T(8,128)S(1)}, u32[]{:S(2)}, u32[]{:S(2)}) collective-permute-start(f32[2,4,64,128]{3,2,1,0:T(8,128)S(1)} %get-tuple-element.1621), channel_id=1, source_target_pairs={{1,0},{2,1},{3,2},{4,3},{5,4},{6,5},{7,6},{8,7},{9,8},{10,9},{11,1... | collective-permute-start | bytes 786440 | tf_op jit(solution)/shard_map/while/body/eval_jaxpr/ppermute | solution.py:18
  516.6 9.8 collective-permute-start.1
  559.2 11.3 %collective-permute-start = (f32[2,4,64,128]{3,2,1,0:T(8,128)S(1)}, f32[2,4,64,128]{3,2,1,0:T(8,128)S(1)}, u32[]{:S(2)}, u32[]{:S(2)}) collective-permute-start(f32[2,4,64,128]{3,2,1,0:T(8,128)S(1)} %get-tuple-element.1621), channel_id=1, source_target_pairs={{1,0},{2,1},{3,2},{4,3},{5,4},{6,5},{7,6},{8,7},{9,8},{10,9},{11,1... | collective-permute-start | bytes 786440 | tf_op jit(solution)/shard_map/while/body/eval_jaxpr/ppermute | solution.py:18
  561.1 9.8 collective-permute-start.1
  603.8 11.3 %collective-permute-start = (f32[2,4,64,128]{3,2,1,0:T(8,128)S(1)}, f32[2,4,64,128]{3,2,1,0:T(8,128)S(1)}, u32[]{:S(2)}, u32[]{:S(2)}) collective-permute-start(f32[2,4,64,128]{3,2,1,0:T(8,128)S(1)} %get-tuple-element.1621), channel_id=1, source_target_pairs={{1,0},{2,1},{3,2},{4,3},{5,4},{6,5},{7,6},{8,7},{9,8},{10,9},{11,1... | collective-permute-start | bytes 786440 | tf_op jit(solution)/shard_map/while/body/eval_jaxpr/ppermute | solution.py:18
  605.7 9.8 collective-permute-start.1
  (383 other events, 1192.6 us)
Sparse Core Ops, SparseCore 0:
  12.6 68.2 all-gather.1
  906.5 111.3 reduce-scatter.4
where the time goes:
time: 1030 us
  other arithmetic  345 us (33%)
  local copies, waits for them, and re-layouts  258 us (25%)
  waiting for transfers between devices  223 us (22%)
  starting transfers between devices  96.6 us (9%)
  blocking collectives  80.6 us (8%)
  between operations  18.5 us (2%)
    while x48, other arithmetic  181 us
    dynamic_update_slice x1, local copies, waits for them, and re-layouts, on_device(): lax.dynamic_update_slice_in_dim(spread, column_grads, lane_start, 3)  157 us
    unnamed x3, waiting for transfers between devices  111 us
    all_to_all x1, blocking collectives, on_device(): lax.all_to_all(padded, 'slab', split_axis=2, concat_axis=1, tiled=True)  80.6 us
    ppermute x12, starting transfers between devices, padded_2(): before = lax.ppermute(last, axis, up)  66.1 us
    all_gather x1, waiting for transfers between devices, on_device(): column = lax.all_gather(owned_model, 'shot', axis=1, tiled=True)  65.2 us
    add x12, other arithmetic, first_along(): summed + centred_first[distance - 1] * (shifted(source_field, along_axis,...  46.8 us
    add x12, other arithmetic, correlate(): return gradients + increments  37.9 us
  transfers between devices with their start and end apart: 27, of which 20 were waited for; matrix products, arithmetic and copies ran while one was open for 1% of the time, Pallas kernels for 0%

commit v1 on v0

v1 whole, which is shorter than its diff:
```python
import functools
import jax
import jax.numpy as jnp
from jax import lax
from jax.sharding import PartitionSpec as P
from jax.experimental import pallas as pl
from jax.experimental.pallas import tpu as pltpu

MESH = pl.DeviceIdType.MESH
F32 = jnp.float32
BF16 = jnp.bfloat16

SECOND = (63.0, -7.875, 1.0, -9.0 / 128.0)
FIRST = (21.0, -5.25, 1.0, -3.0 / 32.0)
UNIT2 = 8.0 / 315.0
UNIT11 = (4.0 / 105.0) ** 2
CENTRE = -7175.0 / 64.0
VMEM_LIMIT = 60 * 1024 * 1024


def second(at):
    total = at(3) + at(-3)
    for k in (1, 2, 4):
        total = total + SECOND[k - 1] * (at(k) + at(-k))
    return total


def first(at):
    total = at(3) - at(-3)
    for k in (1, 2, 4):
        total = total + FIRST[k - 1] * (at(k) - at(-k))
    return total


def sine_cosine(angle):
    u = 0.5 * angle
    w = u * u
    s = 1.0 / 362880.0 - w * (1.0 / 39916800.0)
    for term in (-1.0 / 5040.0, 1.0 / 120.0, -1.0 / 6.0, 1.0):
        s = term + w * s
    s = s * u
    c = -1.0 / 3628800.0 + w * (1.0 / 479001600.0)
    for term in (1.0 / 40320.0, -1.0 / 720.0, 1.0 / 24.0, -0.5, 1.0):
        c = term + w * c
    return 2.0 * s * c, 1.0 - 2.0 * s * s


def where_am_i():
    me_s = lax.axis_index("shot")
    me_b = lax.axis_index("slab")
    half = lax.axis_size("slab") // 2
    return me_s, me_b, half, me_b // half, lax.rem(me_b, half)


def fetch_kernel(v_ref, e_ref, d_ref, t_ref, a_ref, offsets_ref, out_ref,
                 both, sendbuf, psend, precv, send_sem, recv_sem, loc_sem):
    me_s, me_b, half, h, j_me = where_am_i()
    shots = lax.axis_size("shot")
    partner = (me_s, lax.rem(me_b + half, 2 * half))
    target = 2 * me_s + h
    is_self = target == me_b
    not_self = target != me_b
    rows = sendbuf.shape[1] // 5
    src_s, src_h = me_b // 2, lax.rem(me_b, 2)

    barrier = pltpu.get_barrier_semaphore()
    pl.semaphore_signal(barrier, inc=1, device_id=partner, device_id_type=MESH)
    for j in range(half):
        src_b = src_h * half + j

        @pl.when((src_s != me_s) | (src_b != me_b))
        def _():
            pl.semaphore_signal(barrier, inc=1, device_id=(src_s, src_b), device_id_type=MESH)
    pl.semaphore_wait(barrier, 1 + shots - is_self.astype(jnp.int32))

    params = (v_ref, e_ref, d_ref, t_ref, a_ref)
    theirs = pl.ds(pl.multiple_of(rows * (1 - h), 16), rows)
    ours = pl.ds(pl.multiple_of(rows * h, 16), rows)
    swaps = [
        pltpu.make_async_remote_copy(
            src_ref=params[k].at[theirs], dst_ref=both.at[h, k],
            send_sem=psend.at[k], recv_sem=precv.at[k],
            device_id=partner, device_id_type=MESH)
        for k in range(5)
    ]
    for c in swaps:
        c.start()
    for k in range(5):
        both[h, k] = params[k][ours]
    for c in swaps:
        c.wait()

    row_id = lax.broadcasted_iota(jnp.int32, (16, 128), 0)
    residue = j_me * 8 + lax.rem(row_id, 8)
    lane = lax.broadcasted_iota(jnp.int32, (16, 128), 1)

    def outgoing(i):
        s = lax.rem(me_s + i, shots)
        return s, pltpu.make_async_remote_copy(
            src_ref=sendbuf.at[i], dst_ref=out_ref.at[j_me],
            send_sem=send_sem.at[i], recv_sem=recv_sem.at[j_me],
            device_id=(s, target), device_id_type=MESH)

    local = pltpu.make_async_copy(sendbuf.at[0], out_ref.at[j_me], loc_sem)
    for i in range(shots):
        s, copy = outgoing(i)
        upper = residue < offsets_ref[s, 0]
        right = lane < offsets_ref[s, 1]
        for k in range(5):
            @pl.loop(0, rows // 16)
            def _(r):
                at = pl.ds(pl.multiple_of(r * 16, 16), 16)
                lo = both[0, k, at].astype(F32)
                hi = both[1, k, at].astype(F32)
                left_part = jnp.where(upper, hi[:, :128], lo[:, :128])
                right_part = jnp.where(upper, hi[:, 128:], lo[:, 128:])
                sendbuf[i, pl.ds(pl.multiple_of(k * rows + r * 16, 16), 16)] = (
                    jnp.where(right, right_part, left_part).astype(BF16))
        if i == 0:
            @pl.when(not_self)
            def _():
                copy.start()

            @pl.when(is_self)
            def _():
                local.start()
        else:
            copy.start()
    for i in range(shots):
        s, copy = outgoing(i)
        if i == 0:
            @pl.when(not_self)
            def _():
                copy.wait_send()

            @pl.when(is_self)
            def _():
                local.wait()
        else:
            copy.wait_send()
    for j in range(half):
        @pl.when((src_s != me_s) | (src_h * half + j != me_b))
        def _():
            pltpu.make_async_remote_copy(
                src_ref=sendbuf.at[0], dst_ref=out_ref.at[j],
                send_sem=send_sem.at[0], recv_sem=recv_sem.at[j],
                device_id=(src_s, src_h * half + j), device_id_type=MESH).wait_recv()


def return_kernel(g_ref, offsets_ref, out_ref, recv, acc, send_sem, recv_sem, loc_sem, psend, precv):
    me_s, me_b, half, h, j_me = where_am_i()
    shots = lax.axis_size("shot")
    partner = (me_s, lax.rem(me_b + half, 2 * half))
    rows = g_ref.shape[1] // 5
    to_s, to_h = me_b // 2, lax.rem(me_b, 2)
    from_b = 2 * me_s + h
    is_self = from_b == me_b

    barrier = pltpu.get_barrier_semaphore()
    pl.semaphore_signal(barrier, inc=1, device_id=partner, device_id_type=MESH)
    for i in range(shots):
        s = lax.rem(me_s + i, shots)
        if i == 0:
            @pl.when(from_b != me_b)
            def _():
                pl.semaphore_signal(barrier, inc=1, device_id=(s, from_b), device_id_type=MESH)
        else:
            pl.semaphore_signal(barrier, inc=1, device_id=(s, from_b), device_id_type=MESH)
    pl.semaphore_wait(barrier, 1 + half - is_self.astype(jnp.int32))

    def outgoing(i):
        j = lax.rem(j_me + i, half)
        to_b = to_h * half + j
        mine = (to_s == me_s) & (to_b == me_b)
        return mine, j, pltpu.make_async_remote_copy(
            src_ref=g_ref.at[j], dst_ref=recv.at[me_s],
            send_sem=send_sem.at[i], recv_sem=recv_sem.at[me_s],
            device_id=(to_s, to_b), device_id_type=MESH)

    local = pltpu.make_async_copy(g_ref.at[j_me], recv.at[me_s], loc_sem)
    for i in range(half):
        mine, j, copy = outgoing(i)

        @pl.when(jnp.logical_not(mine))
        def _():
            copy.start()
        if i == 0:
            @pl.when(mine)
            def _():
                local.start()

    row_id = lax.broadcasted_iota(jnp.int32, (8, 128), 0)
    residue = j_me * 8 + row_id
    lane = lax.broadcasted_iota(jnp.int32, (8, 128), 1)
    for i in range(shots):
        s = lax.rem(me_s + i, shots)

        def arrive():
            pltpu.make_async_remote_copy(
                src_ref=g_ref.at[0], dst_ref=recv.at[s],
                send_sem=send_sem.at[0], recv_sem=recv_sem.at[s],
                device_id=(s, from_b), device_id_type=MESH).wait_recv()
        if i == 0:
            @pl.when(from_b != me_b)
            def _():
                arrive()

            @pl.when(from_b == me_b)
            def _():
                local.wait()
        else:
            arrive()
        upper = residue < offsets_ref[s, 0]
        right = lane < offsets_ref[s, 1]

        @pl.loop(0, 5 * rows // 8, unroll=4)
        def _(r):
            at = pl.ds(pl.multiple_of(r * 8, 8), 8)
            g = recv[s, at]
            hi = jnp.where(upper, g, 0.0)
            lo = jnp.where(upper, 0.0, g)
            for c, part in ((0, lo), (1, hi)):
                left_part = jnp.where(right, 0.0, part)
                right_part = jnp.where(right, part, 0.0)
                if i == 0:
                    acc[c, at, 0:128] = left_part
                    acc[c, at, 128:256] = right_part
                else:
                    acc[c, at, 0:128] += left_part
                    acc[c, at, 128:256] += right_part
    swaps = []
    for k in range(5):
        swaps.append(pltpu.make_async_remote_copy(
            src_ref=acc.at[1 - h, pl.ds(k * rows, rows)],
            dst_ref=out_ref.at[k, pl.ds(pl.multiple_of(h * rows, 8), rows)],
            send_sem=psend.at[k], recv_sem=precv.at[k],
            device_id=partner, device_id_type=MESH))
        swaps[k].start()
    for k in range(5):
        out_ref[k, pl.ds(pl.multiple_of(h * rows, 8), rows)] = acc[h, k * rows:(k + 1) * rows]
    for c in swaps:
        c.wait()
    for i in range(half):
        mine, j, copy = outgoing(i)

        @pl.when(jnp.logical_not(mine))
        def _():
            copy.wait_send()


def steps_kernel(param_ref, offsets_ref, sources_ref, traces_ref, state_ref, snap_ref, y1_ref,
                 final_ref, g_ref,
                 F, GZ, GY, ZZ, YY, ZY, SF, SG, COEF, ACC, TRIG, dbl, hsend, hrecv):
    me_s, me_b, half, h, j_me = where_am_i()
    slabs = 2 * half
    nz, nx, ny = state_ref.shape[1:]
    nt = snap_ref.shape[0]
    tiles = nx // 16
    ox = lax.rem(offsets_ref[me_s, 0], nx)
    oy = lax.rem(offsets_ref[me_s, 1], ny)
    has_up = me_b > 0
    has_down = me_b < slabs - 1
    up = (me_s, lax.max(me_b - 1, 0))
    down = (me_s, lax.min(me_b + 1, slabs - 1))

    barrier = pltpu.get_barrier_semaphore()

    @pl.when(has_up)
    def _():
        pl.semaphore_signal(barrier, inc=1, device_id=up, device_id_type=MESH)

    @pl.when(has_down)
    def _():
        pl.semaphore_signal(barrier, inc=1, device_id=down, device_id_type=MESH)
    pl.semaphore_wait(barrier, has_up.astype(jnp.int32) + has_down.astype(jnp.int32))

    for slot in range(2):
        for f in range(2):
            @pl.loop(0, nz + 8)
            def _(z):
                F[slot, f, z, 0:8] = jnp.zeros((8, ny), F32)
                F[slot, f, z, 8 + nx:16 + nx] = jnp.zeros((8, ny), F32)

            @pl.when(me_b == 0)
            def _():
                @pl.loop(0, 4)
                def _(z):
                    F[slot, f, z] = jnp.zeros((nx + 16, ny), F32)

            @pl.when(me_b == slabs - 1)
            def _():
                @pl.loop(nz + 4, nz + 8)
                def _(z):
                    F[slot, f, z] = jnp.zeros((nx + 16, ny), F32)

    for f in range(2):
        @pl.loop(0, nz)
        def _(z):
            now = state_ref[f, z]
            F[0, f, z + 4, 8:8 + nx] = now
            F[1, f, z + 4, 8:8 + nx] = state_ref[2 + f, z]
            hi = now.astype(BF16)
            at = pl.ds(pl.multiple_of((f * nz + z) * nx, 16), nx)
            SF[at, 0:ny] = hi
            SF[at, ny:2 * ny] = (now - hi.astype(F32)).astype(BF16)
            for g in (GZ, GY):
                g[f, z, 0:8] = jnp.zeros((8, ny), F32)
                g[f, z, 8 + nx:16 + nx] = jnp.zeros((8, ny), F32)

    def halo(slot, direction):
        rows = (pl.ds(4, 4), pl.ds(nz + 4, 4)) if direction == 0 else (pl.ds(nz, 4), pl.ds(0, 4))
        return pltpu.make_async_remote_copy(
            src_ref=F.at[slot, :, rows[0], pl.ds(8, nx)],
            dst_ref=F.at[slot, :, rows[1], pl.ds(8, nx)],
            send_sem=hsend.at[slot, direction], recv_sem=hrecv.at[slot, direction],
            device_id=(up, down)[direction], device_id_type=MESH)

    def send_halos(slot):
        @pl.when(has_up)
        def _():
            halo(slot, 0).start()

        @pl.when(has_down)
        def _():
            halo(slot, 1).start()

    def wait_halos(slot):
        @pl.when(has_up)
        def _():
            halo(slot, 0).wait_send()
            halo(slot, 1).wait_recv()

        @pl.when(has_down)
        def _():
            halo(slot, 1).wait_send()
            halo(slot, 0).wait_recv()

    send_halos(0)

    lane_shift = lax.rem(ny - oy, ny)
    for k in range(5):
        @pl.loop(0, nz // 2)
        def _(zz):
            for j in range(nx // 8):
                two = param_ref[j, pl.ds(pl.multiple_of(k * nz * 8 + zz * 16, 16), 16)].astype(F32)
                for half_row in range(2):
                    part = two[8 * half_row:8 * half_row + 8]
                    dbl[zz * 2 + half_row, 8 * j:8 * j + 8] = part
                    dbl[zz * 2 + half_row, nx + 8 * j:nx + 8 * j + 8] = part

        @pl.loop(0, nz)
        def _(z):
            TRIG[k, z] = pltpu.roll(dbl[z, pl.ds(ox, nx)], lane_shift, 1)

    source = sources_ref[0]
    first_row = me_b * nz

    @pl.loop(0, nz)
    def _(z):
        for t in range(tiles):
            at = pl.ds(16 * t, 16)
            v = TRIG[0, z, at]
            c = v * v
            a = 1.0 + 2.0 * TRIG[1, z, at]
            b = jnp.sqrt(1.0 + 2.0 * TRIG[2, z, at])
            st, ct = sine_cosine(TRIG[3, z, at])
            sa, ca = sine_cosine(TRIG[4, z, at])
            n_z, n_x, n_y = ct, st * ca, st * sa
            TRIG[1, z, at] = st
            TRIG[2, z, at] = ct
            TRIG[3, z, at] = sa
            TRIG[4, z, at] = ca
            mixed = 2.0 * UNIT11 / UNIT2
            COEF[0, z, at] = n_z * n_z
            COEF[1, z, at] = n_x * n_x
            COEF[2, z, at] = mixed * n_z * n_x
            COEF[3, z, at] = mixed * n_z * n_y
            COEF[4, z, at] = mixed * n_x * n_y
            COEF[5, z, at] = a
            COEF[6, z, at] = b
            COEF[7, z, at] = UNIT2 * c
            cell = (((first_row + z) * nx + 16 * t + lax.broadcasted_iota(jnp.int32, (16, ny), 0)) * ny
                    + lax.broadcasted_iota(jnp.int32, (16, ny), 1))
            COEF[8, z, at] = jnp.where(cell == source, c, 0.0)
            for n in range(8):
                ACC[n, z, at] = jnp.zeros((16, ny), F32)

    def step(t, carry):
        cur = lax.rem(t, 2)
        nxt = 1 - cur
        amplitude = traces_ref[0, t]
        for f in range(2):
            out = jnp.dot(SF[f * nz * nx:(f + 1) * nz * nx], y1_ref[...], preferred_element_type=F32)
            for z in range(nz):
                GY[f, z, 8:8 + nx] = out[z * nx:(z + 1) * nx, 0:ny]
                YY[f, z] = out[z * nx:(z + 1) * nx, ny:2 * ny]
        wait_halos(cur)
        for f in range(2):
            @pl.loop(0, tiles)
            def _(q):
                x0 = pl.multiple_of(8 + 16 * q, 8)
                row = [F[cur, f, z, pl.ds(x0, 16)] for z in range(nz + 8)]
                for z in range(nz):
                    ZZ[f, z, pl.ds(pl.multiple_of(16 * q, 16), 16)] = second(lambda k: row[z + 4 + k])
                    g = first(lambda k: row[z + 4 + k])
                    GZ[f, z, pl.ds(x0, 16)] = g
                    hi = g.astype(BF16)
                    at = pl.ds(pl.multiple_of((f * nz + z) * nx + 16 * q, 16), 16)
                    SG[at, 0:ny] = hi
                    SG[at, ny:2 * ny] = (g - hi.astype(F32)).astype(BF16)
        for f in range(2):
            out = jnp.dot(SG[f * nz * nx:(f + 1) * nz * nx], y1_ref[:, 0:ny], preferred_element_type=F32)
            for z in range(nz):
                ZY[f, z] = out[z * nx:(z + 1) * nx]

        @pl.loop(0, nz)
        def _(z):
            for q in range(tiles):
                at = pl.ds(16 * q, 16)

                def parts(f):
                    def x_of(ref, *lead):
                        return lambda k: ref[(*lead, pl.ds(8 + 16 * q + k, 16))]
                    yy = YY[f, z, at]
                    return (
                        ZZ[f, z, at] - yy,
                        second(x_of(F, cur, f, z + 4)) - yy,
                        first(x_of(GZ, f, z)),
                        ZY[f, z, at],
                        first(x_of(GY, f, z)),
                        yy,
                        F[cur, f, z + 4, pl.ds(8 + 16 * q, 16)],
                    )
                coef = [COEF[n, z, at] for n in range(5)]
                dp = parts(0)
                dq = parts(1)

                def weighted(d):
                    total = coef[0] * d[0]
                    for n in range(1, 5):
                        total = total + coef[n] * d[n]
                    return total
                base_p = dp[5] + CENTRE * dp[6]
                base_q = dq[5] + CENTRE * dq[6]
                h2 = (dp[0] + dp[1]) + (base_p + base_p) - weighted(dp)
                h1 = base_q + weighted(dq)
                a = COEF[5, z, at]
                b = COEF[6, z, at]
                c = COEF[7, z, at]
                pn = (dp[6] + dp[6]) - F[nxt, 0, z + 4, pl.ds(8 + 16 * q, 16)] + c * (a * h2 + b * h1)
                pn = pn + amplitude * COEF[8, z, at]
                qn = (dq[6] + dq[6]) - F[nxt, 1, z + 4, pl.ds(8 + 16 * q, 16)] + c * (b * h2 + h1)
                F[nxt, 0, z + 4, pl.ds(8 + 16 * q, 16)] = pn
                F[nxt, 1, z + 4, pl.ds(8 + 16 * q, 16)] = qn
                for f, value in ((0, pn), (1, qn)):
                    hi = value.astype(BF16)
                    rows = pl.ds(pl.multiple_of((f * nz + z) * nx + 16 * q, 16), 16)
                    SF[rows, 0:ny] = hi
                    SF[rows, ny:2 * ny] = (value - hi.astype(F32)).astype(BF16)
                pf = snap_ref[t, 0, z, at].astype(F32)
                qf = snap_ref[t, 1, z, at].astype(F32)
                bp = b * pf
                wa = a * pf + b * qf
                wb = bp + qf
                ACC[0, z, at] += h2 * wa + h1 * wb
                ACC[1, z, at] += h2 * pf
                ACC[2, z, at] += h1 * pf + h2 * qf
                for n in range(5):
                    ACC[3 + n, z, at] += dq[n] * wb - dp[n] * wa

        @pl.when(t < nt - 1)
        def _():
            send_halos(nxt)
        return carry

    lax.fori_loop(0, nt, step, 0)
    last = nt % 2
    for f in range(2):
        @pl.loop(0, nz)
        def _(z):
            final_ref[f, z] = F[last, f, z + 4, 8:8 + nx]

    back_shift = lax.rem(nx - ox, nx)

    def to_residues(k, value):
        for part in range(2):
            dbl[0, part * nx:(part + 1) * nx] = value
        return pltpu.roll(dbl[0, pl.ds(back_shift, nx)], oy, 1)

    @pl.loop(0, nz)
    def _(z):
        v = TRIG[0, z]
        st, ct, sa, ca = (TRIG[n, z] for n in range(1, 5))
        c = v * v
        b = COEF[6, z]
        n_z, n_x, n_y = ct, st * ca, st * sa
        x = [ACC[n, z] for n in range(8)]
        t_z, t_x, t_y = -st, ct * ca, ct * sa
        a_x, a_y = -st * sa, st * ca
        r = UNIT11 / UNIT2
        tilt = (t_z * n_z * x[3] + t_x * n_x * x[4]
                + r * ((t_z * n_x + t_x * n_z) * x[5] + (t_z * n_y + t_y * n_z) * x[6]
                       + (t_x * n_y + t_y * n_x) * x[7]))
        turn = (a_x * n_x * x[4]
                + r * (a_x * n_z * x[5] + a_y * n_z * x[6] + (a_x * n_y + a_y * n_x) * x[7]))
        sums = (
            2.0 * UNIT2 * v * x[0],
            2.0 * UNIT2 * c * x[1],
            UNIT2 * (c / b) * x[2],
            2.0 * UNIT2 * c * tilt,
            2.0 * UNIT2 * c * turn,
        )
        for k in range(5):
            out = to_residues(k, sums[k])
            for j in range(nx // 8):
                g_ref[j, pl.ds(pl.multiple_of(k * nz * 8 + z * 8, 8), 8)] = out[8 * j:8 * j + 8]


def y_matrix(ny):
    matrix = [[0.0] * (2 * ny) for _ in range(ny)]
    for y in range(ny):
        for k in range(1, 5):
            if y + k < ny:
                matrix[y + k][y] = FIRST[k - 1]
                matrix[y + k][ny + y] = SECOND[k - 1]
            if y - k >= 0:
                matrix[y - k][y] = -FIRST[k - 1]
                matrix[y - k][ny + y] = SECOND[k - 1]
    one = jnp.asarray(matrix, F32).astype(BF16)
    return jnp.concatenate([one, one], axis=0)


def on_device(velocity, epsilon, delta, tilt, azimuth, offsets, sources, traces, adjoint_state, snapshots):
    shots = lax.axis_size("shot")
    slabs = lax.axis_size("slab")
    half = slabs // 2
    _, _, nz, nx, ny = adjoint_state.shape
    nt = snapshots.shape[0]
    depth, width, lanes = velocity.shape
    rows = depth * width // 2
    vmem = pl.BlockSpec(memory_space=pltpu.VMEM)
    smem = pl.BlockSpec(memory_space=pltpu.SMEM)
    dma = pltpu.SemaphoreType.DMA
    params = [m.reshape(depth * width, lanes) for m in (velocity, epsilon, delta, tilt, azimuth)]
    residues = pl.pallas_call(
        fetch_kernel,
        out_shape=jax.ShapeDtypeStruct((half, 5 * rows, lanes // 2), BF16),
        in_specs=[vmem] * 5 + [smem],
        out_specs=vmem,
        scratch_shapes=[
            pltpu.VMEM((2, 5, rows, lanes), BF16),
            pltpu.VMEM((shots, 5 * rows, lanes // 2), BF16),
            dma((5,)), dma((5,)), dma((shots,)), dma((half,)), dma(()),
        ],
        compiler_params=pltpu.CompilerParams(collective_id=0, has_side_effects=True, vmem_limit_bytes=VMEM_LIMIT),
        name="fetch",
    )(*params, offsets)
    state = adjoint_state.reshape(4, nz, nx, ny)
    frames = snapshots.reshape(nt, 2, nz, nx, ny)
    final, sums = pl.pallas_call(
        steps_kernel,
        out_shape=(
            jax.ShapeDtypeStruct((2, nz, nx, ny), F32),
            jax.ShapeDtypeStruct((half, 5 * rows, ny), F32),
        ),
        in_specs=[vmem, smem, smem, smem, vmem, vmem, vmem],
        out_specs=(vmem, vmem),
        scratch_shapes=[
            pltpu.VMEM((2, 2, nz + 8, nx + 16, ny), F32),
            pltpu.VMEM((2, nz, nx + 16, ny), F32),
            pltpu.VMEM((2, nz, nx + 16, ny), F32),
            pltpu.VMEM((2, nz, nx, ny), F32),
            pltpu.VMEM((2, nz, nx, ny), F32),
            pltpu.VMEM((2, nz, nx, ny), F32),
            pltpu.VMEM((2 * nz * nx, 2 * ny), BF16),
            pltpu.VMEM((2 * nz * nx, 2 * ny), BF16),
            pltpu.VMEM((9, nz, nx, ny), F32),
            pltpu.VMEM((8, nz, nx, ny), F32),
            pltpu.VMEM((5, nz, nx, ny), F32),
            pltpu.VMEM((nz, 2 * nx, ny), F32),
            dma((2, 2)), dma((2, 2)),
        ],
        compiler_params=pltpu.CompilerParams(collective_id=1, has_side_effects=True, vmem_limit_bytes=VMEM_LIMIT),
        name="steps",
    )(residues, offsets, sources, traces, state, frames, y_matrix(ny))
    gradients = pl.pallas_call(
        return_kernel,
        out_shape=jax.ShapeDtypeStruct((5, 2 * rows, lanes), F32),
        in_specs=[vmem, smem],
        out_specs=vmem,
        scratch_shapes=[
            pltpu.VMEM((shots, 5 * rows, lanes // 2), F32),
            pltpu.VMEM((2, 5 * rows, lanes), F32),
            dma((half,)), dma((shots,)), dma(()), dma((5,)), dma((5,)),
        ],
        compiler_params=pltpu.CompilerParams(collective_id=2, has_side_effects=True, vmem_limit_bytes=VMEM_LIMIT),
        name="give_back",
    )(sums, offsets)
    return (gradients.reshape(5, depth, width, lanes), final.reshape(2, 1, nz, nx, ny))


def solution(mesh):
    return jax.shard_map(
        on_device,
        mesh=mesh,
        in_specs=(
            P("shot", "slab", None),
            P("shot", "slab", None),
            P("shot", "slab", None),
            P("shot", "slab", None),
            P("shot", "slab", None),
            P(),
            P("shot"),
            P("shot", None),
            P(None, "shot", "slab", None, None),
            P(None, None, "shot", "slab", None, None),
        ),
        out_specs=(P(None, "shot", "slab", None), P(None, "shot", "slab", None, None)),
        check_vma=False,
    )
```

time: 1030 us -> 300 us (0.29)
  the two profiles are of different devices: /device:TPU:80 before, /device:TPU:17 now
where the time goes in v1:
time: 300 us
  Pallas kernels  294 us (98%)
  local copies, waits for them, and re-layouts  4.47 us (1%)
    pallas_call x1, Pallas kernels, on_device(): pl.pallas_call(return_kernel, out_shape=jax.ShapeDtypeStruct((5, 2 * rows...  150 us
    pallas_call x1, Pallas kernels, on_device(): pl.pallas_call(steps_kernel, out_shape=(jax.ShapeDtypeStruct((2, nz, nx,...  116 us
    pallas_call x1, Pallas kernels, on_device(): pl.pallas_call(fetch_kernel, out_shape=jax.ShapeDtypeStruct((half, 5 * ro...  27.7 us

profile of v1, /device:TPU:17, one launch (start us, length us, event | category | flops | bytes accessed | tf_op | source)
XLA Modules:
  0.0 300.0 jit_solution(8805014576714799745)
XLA Ops:
  1.3 1.3 copy.13.offsets_ref
  2.6 27.7 %fetch.1.param_ref = bf16[8,480,128]{2,1,0:T(8,128)(2,1)} custom-call(bf16[192,256]{1,0:T(8,128)(2,1)} %bitcast.15, bf16[192,256]{1,0:T(8,128)(2,1)} %bitcast.16, bf16[192,256]{1,0:T(8,128)(2,1)} %bitcast.17, bf16[192,256]{1,0:T(8,128)(2,1)} %bitcast.18, bf16[192,256]{1,0:T(8,128)(2,1)} %bitcast.19, s32[8,2]{1,0:T(8,128)} %copy.13.offsets_ref), custom_call_target="tpu_custom_call" | custom-call | tf_op jit(solution)/shard_map/fetch/pallas_call | solution.py:545
  30.3 116.5 %steps.1 = (f32[2,12,64,128]{3,2,1,0:T(8,128)}, f32[8,480,128]{2,1,0:T(8,128)}) custom-call(bf16[8,480,128]{2,1,0:T(8,128)(2,1)} %fetch.1.param_ref, s32[8,2]{1,0:T(8,128)} %copy.13.offsets_ref, s32[1]{0:T(128)S(6)} %copy.19.sources_ref, f32[1,12]{1,0:T(1,128)} %traces_ref.1, f32[4,12,64,128]{3,2,1,0:T(8,128)} %bitcast.13, ...), custom_call_target="tpu_custom_call" | custom-call | tf_op jit(solution)/shard_map/steps/pallas_call | solution.py:560
  146.8 0.0 copy-start
  146.8 150.0 %give_back.1 = f32[5,192,256]{2,1,0:T(8,128)} custom-call(f32[8,480,128]{2,1,0:T(8,128)} %get-tuple-element.4.g_ref, s32[8,2]{1,0:T(8,128)} %copy.13.offsets_ref), custom_call_target="tpu_custom_call" | custom-call | tf_op jit(solution)/shard_map/give_back/pallas_call | solution.py:586
  296.8 2.2 copy.20
  299.1 0.0 copy-done
  299.1 0.9 copy.21
Async XLA Ops:
  146.8 152.3 %copy-start = (f32[2,12,64,128]{3,2,1,0:T(8,128)S(1)}, f32[2,12,64,128]{3,2,1,0:T(8,128)}, u32[]{:S(2)}) copy-start(f32[2,12,64,128]{3,2,1,0:T(8,128)} %get-tuple-element.5) | copy-start | bytes 2359300

commit v2 on v1

--- a/solution.py
+++ b/solution.py
@@ -15,6 +15,7 @@
 UNIT2 = 8.0 / 315.0
 UNIT11 = (4.0 / 105.0) ** 2
 CENTRE = -7175.0 / 64.0
+UNROLL = 4
 VMEM_LIMIT = 60 * 1024 * 1024
 
 
@@ -147,105 +148,166 @@
                 device_id=(src_s, src_h * half + j), device_id_type=MESH).wait_recv()
 
 
-def return_kernel(g_ref, offsets_ref, out_ref, recv, acc, send_sem, recv_sem, loc_sem, psend, precv):
+def return_kernel(g_ref, offsets_ref, out_ref, first_in, second_in, third_in, acc,
+                  send_sem, recv_sem, loc_sem, psend, precv):
     me_s, me_b, half, h, j_me = where_am_i()
     shots = lax.axis_size("shot")
     partner = (me_s, lax.rem(me_b + half, 2 * half))
-    rows = g_ref.shape[1] // 5
-    to_s, to_h = me_b // 2, lax.rem(me_b, 2)
-    from_b = 2 * me_s + h
-    is_self = from_b == me_b
+    rows = out_ref.shape[1] // 2
+    x, y_hi, y_lo = me_s // 2, lax.rem(me_s, 2), h
+    z, core = j_me // 2, lax.rem(j_me, 2)
+    columns = shots // 2
 
     barrier = pltpu.get_barrier_semaphore()
-    pl.semaphore_signal(barrier, inc=1, device_id=partner, device_id_type=MESH)
+    count = 0
+    for i in range(1, half):
+        pl.semaphore_signal(barrier, inc=1, device_id=(me_s, y_lo * half + lax.rem(j_me + i, half)),
+                            device_id_type=MESH)
+        count += 1
+    for i in range(1, 4):
+        y = lax.rem(y_hi * 2 + y_lo + i, 4)
+        pl.semaphore_signal(barrier, inc=1, device_id=(x * 2 + y // 2, lax.rem(y, 2) * half + j_me),
+                            device_id_type=MESH)
+        count += 1
+    for i in range(1, columns):
+        pl.semaphore_signal(barrier, inc=1, device_id=(lax.rem(x + i, columns) * 2 + y_hi, me_b),
+                            device_id_type=MESH)
+        count += 1
+    pl.semaphore_wait(barrier, count)
+
+    def remote(stage, i, source, target_slot, device):
+        return pltpu.make_async_remote_copy(
+            src_ref=source, dst_ref=target_slot, send_sem=send_sem.at[stage, i],
+            recv_sem=recv_sem.at[stage, i], device_id=device, device_id_type=MESH)
+
+    def along_z(i):
+        j = lax.rem(j_me + i, half)
+        return pltpu.make_async_remote_copy(
+            src_ref=g_ref.at[j], dst_ref=first_in.at[j_me], send_sem=send_sem.at[0, j],
+            recv_sem=recv_sem.at[0, j_me], device_id=(me_s, y_lo * half + j), device_id_type=MESH)
+
+    own = pltpu.make_async_copy(g_ref.at[j_me], first_in.at[j_me], loc_sem.at[0])
+    own.start()
+    for i in range(1, half):
+        along_z(i).start()
+
+    def along_y(i):
+        j = lax.rem(j_me + i, half)
+        z1, z0, c = j // 4, lax.rem(j // 2, 2), lax.rem(j, 2)
+        slot = (y_hi * 2 + y_lo) * 2 + z1
+        stays = (z0 == y_hi) & (c == y_lo)
+        moves = (z0 != y_hi) | (c != y_lo)
+        go = pltpu.make_async_remote_copy(
+            src_ref=first_in.at[j], dst_ref=second_in.at[slot], send_sem=send_sem.at[1, j],
+            recv_sem=recv_sem.at[1, slot], device_id=(x * 2 + z0, c * half + j_me), device_id_type=MESH)
+        stay = pltpu.make_async_copy(first_in.at[j], second_in.at[slot], loc_sem.at[1 + z1])
+        return stays, moves, go, stay
+
+    for i in range(half):
+        j = lax.rem(j_me + half - i, half)
+        if i == 0:
+            own.wait()
+        else:
+            pltpu.make_async_remote_copy(
+                src_ref=g_ref.at[j], dst_ref=first_in.at[j], send_sem=send_sem.at[0, j],
+                recv_sem=recv_sem.at[0, j], device_id=(me_s, y_lo * half + j), device_id_type=MESH).wait_recv()
+        stays, moves, go, stay = along_y(half - i if i else 0)
+        pl.when(moves)(go.start)
+        pl.when(stays)(stay.start)
+
+    def along_x(i):
+        slot_in = lax.rem((y_hi * 2 + y_lo) * 2 + i, 8)
+        from_hi, from_lo, z1 = slot_in // 4, lax.rem(slot_in // 2, 2), lax.rem(slot_in, 2)
+        to_x = 2 * from_lo + z1
+        shot = x * 2 + from_hi
+        go = pltpu.make_async_remote_copy(
+            src_ref=second_in.at[slot_in], dst_ref=third_in.at[shot], send_sem=send_sem.at[2, slot_in],
+            recv_sem=recv_sem.at[2, shot], device_id=(to_x * 2 + y_hi, me_b), device_id_type=MESH)
+        stay = pltpu.make_async_copy(second_in.at[slot_in], third_in.at[shot], loc_sem.at[3 + from_hi])
+        return to_x == x, to_x != x, go, stay
+
+    def from_y(i):
+        slot_in = lax.rem((y_hi * 2 + y_lo) * 2 + i, 8)
+        from_hi, from_lo, z1 = slot_in // 4, lax.rem(slot_in // 2, 2), lax.rem(slot_in, 2)
+        return pltpu.make_async_remote_copy(
+            src_ref=first_in.at[0], dst_ref=second_in.at[slot_in], send_sem=send_sem.at[1, 0],
+            recv_sem=recv_sem.at[1, slot_in], device_id=(x * 2 + from_hi, from_lo * half + j_me),
+            device_id_type=MESH)
+
+    for i in range(8):
+        if i < 2:
+            slot_in = (y_hi * 2 + y_lo) * 2 + i
+            pltpu.make_async_copy(first_in.at[0], second_in.at[slot_in], loc_sem.at[1 + i]).wait()
+        else:
+            from_y(i).wait_recv()
+        stays, moves, go, stay = along_x(i)
+        pl.when(moves)(go.start)
+        pl.when(stays)(stay.start)
+
     for i in range(shots):
         s = lax.rem(me_s + i, shots)
-        if i == 0:
-            @pl.when(from_b != me_b)
-            def _():
-                pl.semaphore_signal(barrier, inc=1, device_id=(s, from_b), device_id_type=MESH)
-        else:
-            pl.semaphore_signal(barrier, inc=1, device_id=(s, from_b), device_id_type=MESH)
-    pl.semaphore_wait(barrier, 1 + half - is_self.astype(jnp.int32))
-
-    def outgoing(i):
-        j = lax.rem(j_me + i, half)
-        to_b = to_h * half + j
-        mine = (to_s == me_s) & (to_b == me_b)
-        return mine, j, pltpu.make_async_remote_copy(
-            src_ref=g_ref.at[j], dst_ref=recv.at[me_s],
-            send_sem=send_sem.at[i], recv_sem=recv_sem.at[me_s],
-            device_id=(to_s, to_b), device_id_type=MESH)
-
-    local = pltpu.make_async_copy(g_ref.at[j_me], recv.at[me_s], loc_sem)
-    for i in range(half):
-        mine, j, copy = outgoing(i)
-
-        @pl.when(jnp.logical_not(mine))
-        def _():
-            copy.start()
-        if i == 0:
-            @pl.when(mine)
-            def _():
-                local.start()
-
-    row_id = lax.broadcasted_iota(jnp.int32, (8, 128), 0)
-    residue = j_me * 8 + row_id
-    lane = lax.broadcasted_iota(jnp.int32, (8, 128), 1)
-    for i in range(shots):
-        s = lax.rem(me_s + i, shots)
-
-        def arrive():
+        from_hi = lax.rem(s, 2)
+        if i == 0 or i == 1:
+            pass
+        here = s // 2 == x
+        away = s // 2 != x
+
+        @pl.when(here)
+        def _():
+            pltpu.make_async_copy(second_in.at[0], third_in.at[s], loc_sem.at[3 + from_hi]).wait()
+
+        @pl.when(away)
+        def _():
             pltpu.make_async_remote_copy(
-                src_ref=g_ref.at[0], dst_ref=recv.at[s],
-                send_sem=send_sem.at[0], recv_sem=recv_sem.at[s],
-                device_id=(s, from_b), device_id_type=MESH).wait_recv()
-        if i == 0:
-            @pl.when(from_b != me_b)
-            def _():
-                arrive()
-
-            @pl.when(from_b == me_b)
-            def _():
-                local.wait()
-        else:
-            arrive()
-        upper = residue < offsets_ref[s, 0]
-        right = lane < offsets_ref[s, 1]
-
-        @pl.loop(0, 5 * rows // 8, unroll=4)
-        def _(r):
-            at = pl.ds(pl.multiple_of(r * 8, 8), 8)
-            g = recv[s, at]
-            hi = jnp.where(upper, g, 0.0)
-            lo = jnp.where(upper, 0.0, g)
-            for c, part in ((0, lo), (1, hi)):
-                left_part = jnp.where(right, 0.0, part)
-                right_part = jnp.where(right, part, 0.0)
-                if i == 0:
-                    acc[c, at, 0:128] = left_part
-                    acc[c, at, 128:256] = right_part
-                else:
-                    acc[c, at, 0:128] += left_part
-                    acc[c, at, 128:256] += right_part
-    swaps = []
-    for k in range(5):
-        swaps.append(pltpu.make_async_remote_copy(
-            src_ref=acc.at[1 - h, pl.ds(k * rows, rows)],
+                src_ref=second_in.at[0], dst_ref=third_in.at[s], send_sem=send_sem.at[2, 0],
+                recv_sem=recv_sem.at[2, s], device_id=(s // 2 * 2 + y_hi, me_b), device_id_type=MESH).wait_recv()
+
+    row_id = lax.broadcasted_iota(jnp.int32, (16, 128), 0)
+    residue = j_me * 8 + lax.rem(row_id, 8)
+    lane = lax.broadcasted_iota(jnp.int32, (16, 128), 1)
+
+    def swap(k):
+        return pltpu.make_async_remote_copy(
+            src_ref=acc.at[1 - h, k],
             dst_ref=out_ref.at[k, pl.ds(pl.multiple_of(h * rows, 8), rows)],
             send_sem=psend.at[k], recv_sem=precv.at[k],
-            device_id=partner, device_id_type=MESH))
-        swaps[k].start()
+            device_id=partner, device_id_type=MESH)
+
     for k in range(5):
-        out_ref[k, pl.ds(pl.multiple_of(h * rows, 8), rows)] = acc[h, k * rows:(k + 1) * rows]
-    for c in swaps:
-        c.wait()
+        scales, uppers, rights = [], [], []
+        for s in range(shots):
+            exponents = third_in[s, 5 * rows:5 * rows + 16].astype(jnp.int32).astype(F32)
+            scales.append(jnp.broadcast_to(jnp.exp2(exponents[k:k + 1] - 14.9), (16, 128)))
+            uppers.append(residue < offsets_ref[s, 0])
+            rights.append(lane < offsets_ref[s, 1])
+
+        @pl.loop(0, rows // 16)
+        def _(r):
+            at = pl.ds(pl.multiple_of(r * 16, 16), 16)
+            total = [[0.0, 0.0], [0.0, 0.0]]
+            for s in range(shots):
+                g = third_in[s, pl.ds(pl.multiple_of(k * rows + r * 16, 16), 16)].astype(jnp.int32).astype(F32)
+                g = g * scales[s]
+                hi = jnp.where(uppers[s], g, 0.0)
+                for c, part in ((0, g - hi), (1, hi)):
+                    right_part = jnp.where(rights[s], part, 0.0)
+                    total[c][1] = total[c][1] + right_part
+                    total[c][0] = total[c][0] + (part - right_part)
+            for c in range(2):
+                acc[c, k, at, 0:128] = total[c][0]
+                acc[c, k, at, 128:256] = total[c][1]
+        swap(k).start()
+        out_ref[k, pl.ds(pl.multiple_of(h * rows, 8), rows)] = acc[h, k]
+    for k in range(5):
+        swap(k).wait()
+    for i in range(1, half):
+        along_z(i).wait_send()
     for i in range(half):
-        mine, j, copy = outgoing(i)
-
-        @pl.when(jnp.logical_not(mine))
-        def _():
-            copy.wait_send()
+        stays, moves, go, stay = along_y(i)
+        pl.when(moves)(go.wait_send)
+    for i in range(8):
+        stays, moves, go, stay = along_x(i)
+        pl.when(moves)(go.wait_send)
 
 
 def steps_kernel(param_ref, offsets_ref, sources_ref, traces_ref, state_ref, snap_ref, y1_ref,
@@ -307,35 +369,36 @@
                 g[f, z, 0:8] = jnp.zeros((8, ny), F32)
                 g[f, z, 8 + nx:16 + nx] = jnp.zeros((8, ny), F32)
 
-    def halo(slot, direction):
+    def halo(slot, direction, q):
         rows = (pl.ds(4, 4), pl.ds(nz + 4, 4)) if direction == 0 else (pl.ds(nz, 4), pl.ds(0, 4))
         return pltpu.make_async_remote_copy(
-            src_ref=F.at[slot, :, rows[0], pl.ds(8, nx)],
-            dst_ref=F.at[slot, :, rows[1], pl.ds(8, nx)],
-            send_sem=hsend.at[slot, direction], recv_sem=hrecv.at[slot, direction],
+            src_ref=F.at[slot, :, rows[0], pl.ds(8 + 16 * q, 16)],
+            dst_ref=F.at[slot, :, rows[1], pl.ds(8 + 16 * q, 16)],
+            send_sem=hsend.at[slot, direction, q], recv_sem=hrecv.at[slot, direction, q],
             device_id=(up, down)[direction], device_id_type=MESH)
 
-    def send_halos(slot):
+    def send_halos(slot, q):
         @pl.when(has_up)
         def _():
-            halo(slot, 0).start()
+            halo(slot, 0, q).start()
 
         @pl.when(has_down)
         def _():
-            halo(slot, 1).start()
-
-    def wait_halos(slot):
+            halo(slot, 1, q).start()
+
+    def wait_halos(slot, q):
         @pl.when(has_up)
         def _():
-            halo(slot, 0).wait_send()
-            halo(slot, 1).wait_recv()
+            halo(slot, 0, q).wait_send()
+            halo(slot, 1, q).wait_recv()
 
         @pl.when(has_down)
         def _():
-            halo(slot, 1).wait_send()
-            halo(slot, 0).wait_recv()
-
-    send_halos(0)
+            halo(slot, 1, q).wait_send()
+            halo(slot, 0, q).wait_recv()
+
+    for q in range(tiles):
+        send_halos(0, q)
 
     lane_shift = lax.rem(ny - oy, ny)
     for k in range(5):
@@ -385,38 +448,28 @@
             for n in range(8):
                 ACC[n, z, at] = jnp.zeros((16, ny), F32)
 
-    def step(t, carry):
-        cur = lax.rem(t, 2)
-        nxt = 1 - cur
-        amplitude = traces_ref[0, t]
+    def depth_pass(cur, q):
+        wait_halos(cur, q)
         for f in range(2):
-            out = jnp.dot(SF[f * nz * nx:(f + 1) * nz * nx], y1_ref[...], preferred_element_type=F32)
+            row = [F[cur, f, z, 8 + 16 * q:24 + 16 * q] for z in range(nz + 8)]
             for z in range(nz):
-                GY[f, z, 8:8 + nx] = out[z * nx:(z + 1) * nx, 0:ny]
-                YY[f, z] = out[z * nx:(z + 1) * nx, ny:2 * ny]
-        wait_halos(cur)
-        for f in range(2):
-            @pl.loop(0, tiles)
-            def _(q):
-                x0 = pl.multiple_of(8 + 16 * q, 8)
-                row = [F[cur, f, z, pl.ds(x0, 16)] for z in range(nz + 8)]
-                for z in range(nz):
-                    ZZ[f, z, pl.ds(pl.multiple_of(16 * q, 16), 16)] = second(lambda k: row[z + 4 + k])
-                    g = first(lambda k: row[z + 4 + k])
-                    GZ[f, z, pl.ds(x0, 16)] = g
-                    hi = g.astype(BF16)
-                    at = pl.ds(pl.multiple_of((f * nz + z) * nx + 16 * q, 16), 16)
-                    SG[at, 0:ny] = hi
-                    SG[at, ny:2 * ny] = (g - hi.astype(F32)).astype(BF16)
-        for f in range(2):
-            out = jnp.dot(SG[f * nz * nx:(f + 1) * nz * nx], y1_ref[:, 0:ny], preferred_element_type=F32)
-            for z in range(nz):
-                ZY[f, z] = out[z * nx:(z + 1) * nx]
-
-        @pl.loop(0, nz)
-        def _(z):
-            for q in range(tiles):
-                at = pl.ds(16 * q, 16)
+                ZZ[f, z, 16 * q:16 * q + 16] = second(lambda k: row[z + 4 + k])
+                g = first(lambda k: row[z + 4 + k])
+                GZ[f, z, 8 + 16 * q:24 + 16 * q] = g
+                hi = g.astype(BF16)
+                at = (f * nz + z) * 16
+                SG[q, at:at + 16, 0:ny] = hi
+                SG[q, at:at + 16, ny:2 * ny] = (g - hi.astype(F32)).astype(BF16)
+
+    def tile_pass(t, cur, nxt, q, amplitude):
+        ZY[q] = jnp.dot(SG[q], y1_ref[:, 0:ny], preferred_element_type=F32)
+        at = pl.ds(16 * q, 16)
+        inner = pl.ds(8 + 16 * q, 16)
+
+        @pl.loop(0, nz // UNROLL)
+        def _(zz):
+            for z_in in range(UNROLL):
+                z = zz * UNROLL + z_in
 
                 def parts(f):
                     def x_of(ref, *lead):
@@ -426,10 +479,10 @@
                         ZZ[f, z, at] - yy,
                         second(x_of(F, cur, f, z + 4)) - yy,
                         first(x_of(GZ, f, z)),
-                        ZY[f, z, at],
+                        ZY[q, pl.ds(pl.multiple_of((f * nz + z) * 16, 16), 16)],
                         first(x_of(GY, f, z)),
                         yy,
-                        F[cur, f, z + 4, pl.ds(8 + 16 * q, 16)],
+                        F[cur, f, z + 4, inner],
                     )
                 coef = [COEF[n, z, at] for n in range(5)]
                 dp = parts(0)
@@ -447,11 +500,11 @@
                 a = COEF[5, z, at]
                 b = COEF[6, z, at]
                 c = COEF[7, z, at]
-                pn = (dp[6] + dp[6]) - F[nxt, 0, z + 4, pl.ds(8 + 16 * q, 16)] + c * (a * h2 + b * h1)
+                pn = (dp[6] + dp[6]) - F[nxt, 0, z + 4, inner] + c * (a * h2 + b * h1)
                 pn = pn + amplitude * COEF[8, z, at]
-                qn = (dq[6] + dq[6]) - F[nxt, 1, z + 4, pl.ds(8 + 16 * q, 16)] + c * (b * h2 + h1)
-                F[nxt, 0, z + 4, pl.ds(8 + 16 * q, 16)] = pn
-                F[nxt, 1, z + 4, pl.ds(8 + 16 * q, 16)] = qn
+                qn = (dq[6] + dq[6]) - F[nxt, 1, z + 4, inner] + c * (b * h2 + h1)
+                F[nxt, 0, z + 4, inner] = pn
+                F[nxt, 1, z + 4, inner] = qn
                 for f, value in ((0, pn), (1, qn)):
                     hi = value.astype(BF16)
                     rows = pl.ds(pl.multiple_of((f * nz + z) * nx + 16 * q, 16), 16)
@@ -470,7 +523,22 @@
 
         @pl.when(t < nt - 1)
         def _():
-            send_halos(nxt)
+            send_halos(nxt, q)
+
+    def step(t, carry):
+        cur = lax.rem(t, 2)
+        nxt = 1 - cur
+        amplitude = traces_ref[0, t]
+        for f in range(2):
+            out = jnp.dot(SF[f * nz * nx:(f + 1) * nz * nx], y1_ref[...], preferred_element_type=F32)
+            for z in range(nz):
+                GY[f, z, 8:8 + nx] = out[z * nx:(z + 1) * nx, 0:ny]
+                YY[f, z] = out[z * nx:(z + 1) * nx, ny:2 * ny]
+        depth_pass(cur, 0)
+        for q in range(tiles):
+            if q + 1 < tiles:
+                depth_pass(cur, q + 1)
+            tile_pass(t, cur, nxt, q, amplitude)
         return carry
 
     lax.fori_loop(0, nt, step, 0)
@@ -511,9 +579,28 @@
             2.0 * UNIT2 * c * turn,
         )
         for k in range(5):
-            out = to_residues(k, sums[k])
-            for j in range(nx // 8):
-                g_ref[j, pl.ds(pl.multiple_of(k * nz * 8 + z * 8, 8), 8)] = out[8 * j:8 * j + 8]
+            TRIG[k, z] = to_residues(k, sums[k])
+
+    encode(lambda k, z, j: TRIG[k, z, pl.ds(8 * j, 8)], g_ref, nx // 8, nz)
+
+
+def encode(load, out_ref, blocks, nz):
+    for j in range(blocks):
+        exponents = []
+        for k in range(5):
+            largest = jnp.abs(load(k, 0, j))
+            for z in range(1, nz):
+                largest = jnp.maximum(largest, jnp.abs(load(k, z, j)))
+            largest = jnp.max(largest, axis=0, keepdims=True)
+            exponent = jnp.ceil(jnp.log2(jnp.maximum(largest, 1e-30))) + 0.0
+            exponents.append(exponent)
+            scale = jnp.broadcast_to(jnp.exp2(14.9 - exponent), (16, largest.shape[1]))
+            for zz in range(nz // 2):
+                pair = jnp.concatenate([load(k, 2 * zz, j), load(k, 2 * zz + 1, j)], axis=0)
+                at = k * nz * 8 + zz * 16
+                out_ref[j, at:at + 16] = jnp.round(pair * scale).astype(jnp.int32).astype(jnp.int16)
+        rows = jnp.concatenate(exponents + [jnp.zeros_like(exponents[0])] * 11, axis=0)
+        out_ref[j, 5 * nz * 8:5 * nz * 8 + 16] = rows.astype(jnp.int32).astype(jnp.int16)
 
 
 def y_matrix(ny):
@@ -561,7 +648,7 @@
         steps_kernel,
         out_shape=(
             jax.ShapeDtypeStruct((2, nz, nx, ny), F32),
-            jax.ShapeDtypeStruct((half, 5 * rows, ny), F32),
+            jax.ShapeDtypeStruct((half, 5 * rows + 16, ny), jnp.int16),
         ),
         in_specs=[vmem, smem, smem, smem, vmem, vmem, vmem],
         out_specs=(vmem, vmem),
@@ -571,14 +658,14 @@
             pltpu.VMEM((2, nz, nx + 16, ny), F32),
             pltpu.VMEM((2, nz, nx, ny), F32),
             pltpu.VMEM((2, nz, nx, ny), F32),
-            pltpu.VMEM((2, nz, nx, ny), F32),
+            pltpu.VMEM((nx // 16, 2 * nz * 16, ny), F32),
             pltpu.VMEM((2 * nz * nx, 2 * ny), BF16),
-            pltpu.VMEM((2 * nz * nx, 2 * ny), BF16),
+            pltpu.VMEM((nx // 16, 2 * nz * 16, 2 * ny), BF16),
             pltpu.VMEM((9, nz, nx, ny), F32),
             pltpu.VMEM((8, nz, nx, ny), F32),
             pltpu.VMEM((5, nz, nx, ny), F32),
             pltpu.VMEM((nz, 2 * nx, ny), F32),
-            dma((2, 2)), dma((2, 2)),
+            dma((2, 2, nx // 16)), dma((2, 2, nx // 16)),
         ],
         compiler_params=pltpu.CompilerParams(collective_id=1, has_side_effects=True, vmem_limit_bytes=VMEM_LIMIT),
         name="steps",
@@ -589,9 +676,11 @@
         in_specs=[vmem, smem],
         out_specs=vmem,
         scratch_shapes=[
-            pltpu.VMEM((shots, 5 * rows, lanes // 2), F32),
-            pltpu.VMEM((2, 5 * rows, lanes), F32),
-            dma((half,)), dma((shots,)), dma(()), dma((5,)), dma((5,)),
+            pltpu.VMEM((half, 5 * rows + 16, ny), jnp.int16),
+            pltpu.VMEM((8, 5 * rows + 16, ny), jnp.int16),
+            pltpu.VMEM((shots, 5 * rows + 16, ny), jnp.int16),
+            pltpu.VMEM((2, 5, rows, lanes), F32),
+            dma((3, 8)), dma((3, 8)), dma((5,)), dma((5,)), dma((5,)),
         ],
         compiler_params=pltpu.CompilerParams(collective_id=2, has_side_effects=True, vmem_limit_bytes=VMEM_LIMIT),
         name="give_back",

time: 300 us -> 173 us (0.58)
  the two profiles are of different devices: /device:TPU:17 before, /device:TPU:2 now
where the time goes in v2:
time: 173 us; the launch traced here: 172 us
  Pallas kernels  165 us (95%)
  local copies, waits for them, and re-layouts  5.68 us (3%)
    pallas_call x1, Pallas kernels, on_device(): pl.pallas_call(steps_kernel, out_shape=(jax.ShapeDtypeStruct((2, nz, nx,...  67.6 us
    pallas_call x1, Pallas kernels, on_device(): pl.pallas_call(return_kernel, out_shape=jax.ShapeDtypeStruct((5, 2 * rows...  63.6 us
    pallas_call x1, Pallas kernels, on_device(): pl.pallas_call(fetch_kernel, out_shape=jax.ShapeDtypeStruct((half, 5 * ro...  34.2 us
    unnamed x3, local copies, waits for them, and re-layouts  5.68 us

profile of v2, /device:TPU:2, one launch (start us, length us, event | category | flops | bytes accessed | tf_op | source)
XLA Modules:
  0.0 172.3 jit_solution(2825701646995759296)
XLA Ops:
  1.3 1.3 copy.13.offsets_ref
  2.6 34.2 %fetch.1.param_ref = bf16[8,480,128]{2,1,0:T(8,128)(2,1)} custom-call(bf16[192,256]{1,0:T(8,128)(2,1)} %bitcast.15, bf16[192,256]{1,0:T(8,128)(2,1)} %bitcast.16, bf16[192,256]{1,0:T(8,128)(2,1)} %bitcast.17, bf16[192,256]{1,0:T(8,128)(2,1)} %bitcast.18, bf16[192,256]{1,0:T(8,128)(2,1)} %bitcast.19, s32[8,2]{1,0:T(8,128)} %copy.13.offsets_ref), custom_call_target="tpu_custom_call" | custom-call | tf_op jit(solution)/shard_map/fetch/pallas_call | solution.py:632
  36.8 67.6 %steps.1 = (f32[2,12,64,128]{3,2,1,0:T(8,128)}, s16[8,496,128]{2,1,0:T(8,128)(2,1)}) custom-call(bf16[8,480,128]{2,1,0:T(8,128)(2,1)} %fetch.1.param_ref, s32[8,2]{1,0:T(8,128)} %copy.13.offsets_ref, s32[1]{0:T(128)S(6)} %copy.19.sources_ref, f32[1,12]{1,0:T(1,128)} %traces_ref.1, f32[4,12,64,128]{3,2,1,0:T(8,128)} %bitcast.13, ...), custom_call_target="tpu_custom_call" | custom-call | tf_op jit(solution)/shard_map/steps/pallas_call | solution.py:647
  104.4 63.6 %give_back.1 = f32[5,192,256]{2,1,0:T(8,128)} custom-call(s16[8,496,128]{2,1,0:T(8,128)(2,1)} %get-tuple-element.4.g_ref, s32[8,2]{1,0:T(8,128)} %copy.13.offsets_ref), custom_call_target="tpu_custom_call" | custom-call | tf_op jit(solution)/shard_map/give_back/pallas_call | solution.py:673
  168.0 2.2 %copy.20 = f32[5,24,8,256]{3,2,1,0:T(8,128)} copy(f32[5,24,8,256]{3,2,1,0:T(8,128)} %bitcast.12) | data formatting | bytes 1966080
  170.2 2.1 %copy.21 = f32[2,1,12,64,128]{4,3,2,1,0:T(8,128)} copy(f32[2,1,12,64,128]{4,3,2,1,0:T(8,128)} %bitcast.14) | data formatting | bytes 1572864

commit v3 on v1

v3 whole, which is shorter than its diff:
```python
import functools
import jax
import jax.numpy as jnp
from jax import lax
from jax.sharding import PartitionSpec as P
from jax.experimental import pallas as pl
from jax.experimental.pallas import tpu as pltpu

MESH = pl.DeviceIdType.MESH
F32 = jnp.float32
BF16 = jnp.bfloat16

SECOND = (63.0, -7.875, 1.0, -9.0 / 128.0)
FIRST = (21.0, -5.25, 1.0, -3.0 / 32.0)
UNIT2 = 8.0 / 315.0
UNIT11 = (4.0 / 105.0) ** 2
CENTRE = -7175.0 / 64.0
EXPONENT_ROWS = 16
VMEM_LIMIT = 60 * 1024 * 1024


def second(at):
    total = at(3) + at(-3)
    for k in (1, 2, 4):
        total = total + SECOND[k - 1] * (at(k) + at(-k))
    return total


def first(at):
    total = at(3) - at(-3)
    for k in (1, 2, 4):
        total = total + FIRST[k - 1] * (at(k) - at(-k))
    return total


def sine_cosine(angle):
    u = 0.5 * angle
    w = u * u
    s = 1.0 / 362880.0 - w * (1.0 / 39916800.0)
    for term in (-1.0 / 5040.0, 1.0 / 120.0, -1.0 / 6.0, 1.0):
        s = term + w * s
    s = s * u
    c = -1.0 / 3628800.0 + w * (1.0 / 479001600.0)
    for term in (1.0 / 40320.0, -1.0 / 720.0, 1.0 / 24.0, -0.5, 1.0):
        c = term + w * c
    return 2.0 * s * c, 1.0 - 2.0 * s * s


def where_am_i():
    me_s = lax.axis_index("shot")
    me_b = lax.axis_index("slab")
    half = lax.axis_size("slab") // 2
    return me_s, me_b, half, me_b // half, lax.rem(me_b, half)


def remote(source, target, send, recv, device):
    return pltpu.make_async_remote_copy(
        src_ref=source, dst_ref=target, send_sem=send, recv_sem=recv, device_id=device, device_id_type=MESH)


def whole_kernel(v_ref, e_ref, d_ref, t_ref, a_ref, offsets_ref, sources_ref, traces_ref, state_ref, snap_hbm, y1_ref,
                 final_ref, out_ref,
                 both, sendbuf, pin, F, GZ, GY, ZZ, YY, ZY, SF, SG, COEF, ACC, TRIG, dbl, SNAP, MX,
                 GQ, first_in, second_in, third_in, acc, swap_out, swap_in,
                 in_sem, psend, precv, asend, arecv, aloc, hsend, hrecv, rsend, rrecv, rloc, ssend, srecv):
    me_s, me_b, half, h, j_me = where_am_i()
    shots = lax.axis_size("shot")
    slabs = 2 * half
    nz, nx, ny = state_ref.shape[1:]
    nt = SNAP.shape[0]
    tiles = nx // 16
    rows = nz * 8
    block = 2 * nz * 16
    partner = (me_s, lax.rem(me_b + half, slabs))
    x, y_hi, y_lo = me_s // 2, lax.rem(me_s, 2), h
    y_me = y_hi * 2 + y_lo
    columns = shots // 2

    target = 2 * me_s + h
    src_s, src_h = me_b // 2, lax.rem(me_b, 2)
    is_self = target == me_b
    not_self = target != me_b
    has_up = me_b > 0
    has_down = me_b < slabs - 1
    up = (me_s, lax.max(me_b - 1, 0))
    down = (me_s, lax.min(me_b + 1, slabs - 1))

    def z_line(i):
        return (me_s, y_lo * half + lax.rem(j_me + i, half))

    def y_line(i):
        y = lax.rem(y_me + i, 4)
        return (x * 2 + y // 2, lax.rem(y, 2) * half + j_me)

    def x_line(i):
        return (lax.rem(x + i, columns) * 2 + y_hi, me_b)

    barrier = pltpu.get_barrier_semaphore()

    def greet(device):
        pl.semaphore_signal(barrier, inc=1, device_id=device, device_id_type=MESH)

    for i in range(1, half):
        greet(z_line(i))
    for i in range(1, 4):
        greet(y_line(i))
    for i in range(1, columns):
        greet(x_line(i))
    pl.when(has_up)(lambda: greet(up))
    pl.when(has_down)(lambda: greet(down))
    for j in range(half):
        pl.when((src_s != me_s) | (src_h * half + j != me_b))(lambda: greet((src_s, src_h * half + j)))

    loads = [pltpu.make_async_copy(state_ref.at[n], F.at[n // 2, n % 2, pl.ds(4, nz), pl.ds(8, nx)], in_sem.at[n])
             for n in range(4)]
    loads.append(pltpu.make_async_copy(snap_hbm, SNAP, in_sem.at[4]))
    for c in loads:
        c.start()

    @pl.loop(0, nz + 8)
    def _(z):
        for slot in range(2):
            for f in range(2):
                F[slot, f, z, 0:8] = jnp.zeros((8, ny), F32)
                F[slot, f, z, 8 + nx:16 + nx] = jnp.zeros((8, ny), F32)

    @pl.loop(0, nz)
    def _(z):
        for f in range(2):
            for g in (GZ, GY.at[0], GY.at[1]):
                g[f, z, 0:8] = jnp.zeros((8, ny), F32)
                g[f, z, 8 + nx:16 + nx] = jnp.zeros((8, ny), F32)

    def clear(first_row):
        @pl.loop(0, 4)
        def _(z):
            for slot in range(2):
                for f in range(2):
                    F[slot, f, first_row + z] = jnp.zeros((nx + 16, ny), F32)

    pl.when(me_b == 0)(lambda: clear(0))
    pl.when(me_b == slabs - 1)(lambda: clear(nz + 4))

    pl.semaphore_wait(barrier, (half - 1) + 3 + (columns - 1) + has_up.astype(jnp.int32) + has_down.astype(jnp.int32)
                      + shots - is_self.astype(jnp.int32))

    params = (v_ref, e_ref, d_ref, t_ref, a_ref)
    theirs = pl.ds(pl.multiple_of(rows * (1 - h), 16), rows)
    ours = pl.ds(pl.multiple_of(rows * h, 16), rows)
    swaps = [remote(params[k].at[theirs], both.at[h, k], psend.at[k], precv.at[k], partner) for k in range(5)]
    for c in swaps:
        c.start()
    for k in range(5):
        both[h, k] = params[k][ours]

    def halo(slot, direction, q):
        rows = (pl.ds(4, 4), pl.ds(nz + 4, 4)) if direction == 0 else (pl.ds(nz, 4), pl.ds(0, 4))
        return remote(F.at[slot, :, rows[0], pl.ds(8 + 16 * q, 16)], F.at[slot, :, rows[1], pl.ds(8 + 16 * q, 16)],
                      hsend.at[slot, direction, q], hrecv.at[slot, direction, q], (up, down)[direction])

    def send_halos(slot, q):
        pl.when(has_up)(lambda: halo(slot, 0, q).start())
        pl.when(has_down)(lambda: halo(slot, 1, q).start())

    def wait_halos(slot, q):
        @pl.when(has_up)
        def _():
            halo(slot, 0, q).wait_send()
            halo(slot, 1, q).wait_recv()

        @pl.when(has_down)
        def _():
            halo(slot, 1, q).wait_send()
            halo(slot, 0, q).wait_recv()

    row_id = lax.broadcasted_iota(jnp.int32, (16, 128), 0)
    residue = j_me * 8 + lax.rem(row_id, 8)
    lane = lax.broadcasted_iota(jnp.int32, (16, 128), 1)

    def outgoing(i, k):
        s = lax.rem(me_s + i, shots)
        return remote(sendbuf.at[i, k], pin.at[j_me, k], asend.at[i, k], arecv.at[j_me, k], (s, target))

    def local(k):
        return pltpu.make_async_copy(sendbuf.at[0, k], pin.at[j_me, k], aloc.at[k])

    for k in range(5):
        swaps[k].wait()

        @pl.loop(0, rows // 16)
        def _(r):
            at = pl.ds(pl.multiple_of(r * 16, 16), 16)
            lo = both[0, k, at].astype(F32)
            hi = both[1, k, at].astype(F32)
            for i in range(shots):
                s = lax.rem(me_s + i, shots)
                upper = residue < offsets_ref[0, s]
                right = lane < offsets_ref[1, s]
                left_part = jnp.where(upper, hi[:, :128], lo[:, :128])
                right_part = jnp.where(upper, hi[:, 128:], lo[:, 128:])
                sendbuf[i, k, at] = jnp.where(right, right_part, left_part).astype(BF16)
        pl.when(not_self)(lambda: outgoing(0, k).start())
        pl.when(is_self)(lambda: local(k).start())
        for i in range(1, shots):
            outgoing(i, k).start()

    for c in loads[:4]:
        c.wait()
    for q in range(tiles):
        send_halos(0, q)

    def split(value, store):
        hi = value.astype(BF16)
        store(slice(0, ny), hi)
        store(slice(ny, 2 * ny), (value - hi.astype(F32)).astype(BF16))

    def along_y(slot, q):
        out = jnp.dot(SF[q], y1_ref[...], preferred_element_type=F32)
        for f in range(2):
            for z in range(nz):
                at = (f * nz + z) * 16
                GY[slot, f, z, 8 + 16 * q:24 + 16 * q] = out[at:at + 16, 0:ny]
                YY[slot, f, z, 16 * q:16 * q + 16] = out[at:at + 16, ny:2 * ny]

    for q in range(tiles):
        for f in range(2):
            @pl.loop(0, nz)
            def _(z):
                at = pl.ds(pl.multiple_of((f * nz + z) * 16, 16), 16)

                def store(lanes, value):
                    SF[q, at, lanes] = value
                split(F[0, f, z + 4, 8 + 16 * q:24 + 16 * q], store)
    for q in range(tiles - 1):
        along_y(0, q)

    ox = lax.rem(offsets_ref[0, me_s], nx)
    oy = lax.rem(offsets_ref[1, me_s], ny)
    lane_shift = lax.rem(ny - oy, ny)
    for k in range(5):
        for j in range(half):
            here = is_self & (j_me == j)
            away = not_self | (j_me != j)
            pl.when(here)(lambda: local(k).wait())
            pl.when(away)(lambda: remote(sendbuf.at[0, k], pin.at[j, k], asend.at[0, k], arecv.at[j, k],
                                         (src_s, src_h * half + j)).wait_recv())

        @pl.loop(0, nz // 2)
        def _(zz):
            for j in range(half):
                two = pin[j, k, pl.ds(pl.multiple_of(zz * 16, 16), 16)].astype(F32)
                for half_row in range(2):
                    part = two[8 * half_row:8 * half_row + 8]
                    dbl[zz * 2 + half_row, 8 * j:8 * j + 8] = part
                    dbl[zz * 2 + half_row, nx + 8 * j:nx + 8 * j + 8] = part

        @pl.loop(0, nz)
        def _(z):
            TRIG[k, z] = pltpu.roll(dbl[z, pl.ds(ox, nx)], lane_shift, 1)

    source = sources_ref[0]
    first_row = me_b * nz

    @pl.loop(0, nz)
    def _(z):
        for t in range(tiles):
            at = pl.ds(16 * t, 16)
            v = TRIG[0, z, at]
            c = v * v
            a = 1.0 + 2.0 * TRIG[1, z, at]
            b = jnp.sqrt(1.0 + 2.0 * TRIG[2, z, at])
            st, ct = sine_cosine(TRIG[3, z, at])
            sa, ca = sine_cosine(TRIG[4, z, at])
            n_z, n_x, n_y = ct, st * ca, st * sa
            TRIG[1, z, at] = st
            TRIG[2, z, at] = ct
            TRIG[3, z, at] = sa
            TRIG[4, z, at] = ca
            mixed = 2.0 * UNIT11 / UNIT2
            COEF[0, z, at] = n_z * n_z
            COEF[1, z, at] = n_x * n_x
            COEF[2, z, at] = mixed * n_z * n_x
            COEF[3, z, at] = mixed * n_z * n_y
            COEF[4, z, at] = mixed * n_x * n_y
            COEF[5, z, at] = a
            COEF[6, z, at] = b
            COEF[7, z, at] = UNIT2 * c
            cell = (((first_row + z) * nx + 16 * t + lax.broadcasted_iota(jnp.int32, (16, ny), 0)) * ny
                    + lax.broadcasted_iota(jnp.int32, (16, ny), 1))
            COEF[8, z, at] = jnp.where(cell == source, c, 0.0)
            for n in range(8):
                ACC[n, z, at] = jnp.zeros((16, ny), F32)

    loads[4].wait()

    def depth_pass(cur, q):
        for f in range(2):
            row = [F[cur, f, z, 8 + 16 * q:24 + 16 * q] for z in range(nz + 8)]
            for z in range(nz):
                ZZ[f, z, 16 * q:16 * q + 16] = second(lambda k: row[z + 4 + k])
                g = first(lambda k: row[z + 4 + k])
                GZ[f, z, 8 + 16 * q:24 + 16 * q] = g
                at = (f * nz + z) * 16

                def store(lanes, value):
                    SG[q, at:at + 16, lanes] = value
                split(g, store)

    def update(t, cur, nxt, q, z, amplitude):
        at = pl.ds(16 * q, 16)
        inner = pl.ds(8 + 16 * q, 16)

        def parts(f):
            def x_of(ref, *lead):
                return lambda k: ref[(*lead, pl.ds(8 + 16 * q + k, 16))]
            yy = YY[cur, f, z, at]
            return (
                ZZ[f, z, at] - yy,
                second(x_of(F, cur, f, z + 4)) - yy,
                first(x_of(GZ, f, z)),
                ZY[q, pl.ds(pl.multiple_of((f * nz + z) * 16, 16), 16)],
                first(x_of(GY, cur, f, z)),
                yy,
                F[cur, f, z + 4, inner],
            )
        coef = [COEF[n, z, at] for n in range(5)]
        dp = parts(0)
        dq = parts(1)

        def weighted(d):
            total = coef[0] * d[0]
            for n in range(1, 5):
                total = total + coef[n] * d[n]
            return total
        base_p = dp[5] + CENTRE * dp[6]
        base_q = dq[5] + CENTRE * dq[6]
        h2 = (dp[0] + dp[1]) + (base_p + base_p) - weighted(dp)
        h1 = base_q + weighted(dq)
        a = COEF[5, z, at]
        b = COEF[6, z, at]
        c = COEF[7, z, at]
        pn = (dp[6] + dp[6]) - F[nxt, 0, z + 4, inner] + c * (a * h2 + b * h1)
        pn = pn + amplitude * COEF[8, z, at]
        qn = (dq[6] + dq[6]) - F[nxt, 1, z + 4, inner] + c * (b * h2 + h1)
        F[nxt, 0, z + 4, inner] = pn
        F[nxt, 1, z + 4, inner] = qn
        for f, value in ((0, pn), (1, qn)):
            def store(lanes, part):
                SF[q, pl.ds(pl.multiple_of((f * nz + z) * 16, 16), 16), lanes] = part
            split(value, store)
        pf = SNAP[t, 0, z, at].astype(F32)
        qf = SNAP[t, 1, z, at].astype(F32)
        bp = b * pf
        wa = a * pf + b * qf
        wb = bp + qf
        ACC[0, z, at] += h2 * wa + h1 * wb
        ACC[1, z, at] += h2 * pf
        ACC[2, z, at] += h1 * pf + h2 * qf
        for n in range(5):
            ACC[3 + n, z, at] += dq[n] * wb - dp[n] * wa

    def step(t, carry):
        cur = lax.rem(t, 2)
        nxt = 1 - cur
        amplitude = traces_ref[0, t]
        wait_halos(cur, 0)
        along_y(cur, tiles - 1)
        depth_pass(cur, 0)
        for q in range(tiles):
            if q + 1 < tiles:
                wait_halos(cur, q + 1)
                depth_pass(cur, q + 1)
            ZY[q] = jnp.dot(SG[q], y1_ref[:, 0:ny], preferred_element_type=F32)
            if q > 0:
                along_y(nxt, q - 1)

            @pl.loop(0, 2)
            def _(zz):
                for z in range(4):
                    update(t, cur, nxt, q, zz * 8 + z, amplitude)
            pl.when(t < nt - 1)(lambda: send_halos(nxt, q))
            for z in range(4, 8):
                update(t, cur, nxt, q, z, amplitude)
        return carry

    lax.fori_loop(0, nt, step, 0)
    last = nt % 2
    for f in range(2):
        @pl.loop(0, nz)
        def _(z):
            final_ref[f, z] = F[last, f, z + 4, 8:8 + nx]

    back_shift = lax.rem(nx - ox, nx)
    MX[...] = jnp.zeros_like(MX)

    @pl.loop(0, nz)
    def _(z):
        v = TRIG[0, z]
        st, ct, sa, ca = (TRIG[n, z] for n in range(1, 5))
        c = v * v
        b = COEF[6, z]
        n_z, n_x, n_y = ct, st * ca, st * sa
        g = [ACC[n, z] for n in range(8)]
        t_z, t_x, t_y = -st, ct * ca, ct * sa
        a_x, a_y = -st * sa, st * ca
        r = UNIT11 / UNIT2
        tilt = (t_z * n_z * g[3] + t_x * n_x * g[4]
                + r * ((t_z * n_x + t_x * n_z) * g[5] + (t_z * n_y + t_y * n_z) * g[6]
                       + (t_x * n_y + t_y * n_x) * g[7]))
        turn = (a_x * n_x * g[4]
                + r * (a_x * n_z * g[5] + a_y * n_z * g[6] + (a_x * n_y + a_y * n_x) * g[7]))
        sums = (
            2.0 * UNIT2 * v * g[0],
            2.0 * UNIT2 * c * g[1],
            UNIT2 * (c / b) * g[2],
            2.0 * UNIT2 * c * tilt,
            2.0 * UNIT2 * c * turn,
        )
        for k in range(5):
            for part in range(2):
                dbl[k, part * nx:(part + 1) * nx] = sums[k]
        for k in range(5):
            value = pltpu.roll(dbl[k, pl.ds(back_shift, nx)], oy, 1)
            TRIG[k, z] = value
            MX[k] = jnp.maximum(MX[k], jnp.abs(value))

    def exponent_of(largest):
        return jnp.ceil(jnp.log2(jnp.maximum(jnp.max(largest, axis=0, keepdims=True), 1e-30)))

    def exponent_rows(exponents):
        rest = [jnp.zeros_like(exponents[0])] * (EXPONENT_ROWS - len(exponents))
        return jnp.concatenate(exponents + rest, axis=0).astype(jnp.int32).astype(jnp.int16)

    def coded(value):
        return jnp.round(value).astype(jnp.int32).astype(jnp.int16)

    for j in range(half):
        exponents = []
        for k in range(5):
            exponents.append(exponent_of(MX[k, 8 * j:8 * j + 8]))
            MX[k, 8 * j:8 * j + 8] = jnp.broadcast_to(jnp.exp2(14.9 - exponents[k]), (8, ny))
        GQ[j, 0:EXPONENT_ROWS] = exponent_rows(exponents)

    def chunk(k):
        return pl.ds(0, EXPONENT_ROWS + rows) if k == 0 else pl.ds(EXPONENT_ROWS + k * rows, rows)

    def hop_z(k, i):
        j = lax.rem(j_me + i, half)
        return remote(GQ.at[j, chunk(k)], first_in.at[j_me, chunk(k)], rsend.at[0, k, j], rrecv.at[0, k, j_me],
                      (me_s, y_lo * half + j))

    def own_z(k):
        return pltpu.make_async_copy(GQ.at[j_me, chunk(k)], first_in.at[j_me, chunk(k)], rloc.at[k, 0])

    for k in range(5):
        @pl.loop(0, nz // 2)
        def _(zz):
            for j in range(half):
                scale = MX[k, 8 * j:8 * j + 8]
                pair = jnp.concatenate([TRIG[k, 2 * zz, 8 * j:8 * j + 8] * scale,
                                        TRIG[k, 2 * zz + 1, 8 * j:8 * j + 8] * scale], axis=0)
                GQ[j, pl.ds(pl.multiple_of(EXPONENT_ROWS + k * rows + zz * 16, 16), 16)] = coded(pair)
        own_z(k).start()
        for i in range(1, half):
            hop_z(k, i).start()

    def hop_y(k, i):
        j = lax.rem(j_me + i, half)
        z1, z0, c = j // 4, lax.rem(j // 2, 2), lax.rem(j, 2)
        slot = y_me * 2 + z1
        go = remote(first_in.at[j, chunk(k)], second_in.at[slot, chunk(k)], rsend.at[1, k, j], rrecv.at[1, k, slot],
                    (x * 2 + z0, c * half + j_me))
        stay = pltpu.make_async_copy(first_in.at[j, chunk(k)], second_in.at[slot, chunk(k)], rloc.at[k, 1 + z1])
        return (z0 == y_hi) & (c == y_lo), (z0 != y_hi) | (c != y_lo), go, stay

    def forward_y(k):
        for i in range(half):
            j = lax.rem(j_me + i, half)
            if i == 0:
                own_z(k).wait()
            else:
                remote(GQ.at[j, chunk(k)], first_in.at[j, chunk(k)], rsend.at[0, k, j], rrecv.at[0, k, j],
                       (me_s, y_lo * half + j)).wait_recv()
            stays, moves, go, stay = hop_y(k, i)
            pl.when(moves)(go.start)
            pl.when(stays)(stay.start)

    def hop_x(k, i):
        slot = lax.rem(y_me * 2 + i, 8)
        from_hi, from_lo, z1 = slot // 4, lax.rem(slot // 2, 2), lax.rem(slot, 2)
        to_x = 2 * from_lo + z1
        shot = x * 2 + from_hi
        go = remote(second_in.at[slot, chunk(k)], third_in.at[shot, chunk(k)], rsend.at[2, k, slot],
                    rrecv.at[2, k, shot], (to_x * 2 + y_hi, me_b))
        stay = pltpu.make_async_copy(second_in.at[slot, chunk(k)], third_in.at[shot, chunk(k)],
                                     rloc.at[k, 3 + from_hi])
        return to_x == x, to_x != x, go, stay

    def forward_x(k):
        for i in range(8):
            slot = lax.rem(y_me * 2 + i, 8)
            if i < 2:
                pltpu.make_async_copy(first_in.at[0, chunk(k)], second_in.at[slot, chunk(k)], rloc.at[k, 1 + i]).wait()
            else:
                from_hi, from_lo = slot // 4, lax.rem(slot // 2, 2)
                remote(first_in.at[0, chunk(k)], second_in.at[slot, chunk(k)], rsend.at[1, k, 0],
                       rrecv.at[1, k, slot], (x * 2 + from_hi, from_lo * half + j_me)).wait_recv()
            stays, moves, go, stay = hop_x(k, i)
            pl.when(moves)(go.start)
            pl.when(stays)(stay.start)

    def swap(k):
        return remote(swap_out.at[k], swap_in.at[k], ssend.at[k], srecv.at[k], partner)

    def gather(k):
        for i in range(shots):
            s = lax.rem(me_s + i, shots)
            here = s // 2 == x
            away = s // 2 != x
            pl.when(here)(lambda: pltpu.make_async_copy(
                second_in.at[0, chunk(k)], third_in.at[s, chunk(k)], rloc.at[k, 3 + lax.rem(s, 2)]).wait())
            pl.when(away)(lambda: remote(
                second_in.at[0, chunk(k)], third_in.at[s, chunk(k)], rsend.at[2, k, 0], rrecv.at[2, k, s],
                (s // 2 * 2 + y_hi, me_b)).wait_recv())
        scales = []
        for s in range(shots):
            exponents = third_in[s, 0:EXPONENT_ROWS].astype(jnp.int32).astype(F32)
            scales.append(jnp.broadcast_to(jnp.exp2(exponents[k:k + 1] - 14.9), (16, 128)))

        @pl.loop(0, rows // 16)
        def _(r):
            at = pl.ds(pl.multiple_of(r * 16, 16), 16)
            total = [[0.0, 0.0], [0.0, 0.0]]
            for s in range(shots):
                upper = residue < offsets_ref[0, s]
                right = lane < offsets_ref[1, s]
                g = third_in[s, pl.ds(pl.multiple_of(EXPONENT_ROWS + k * rows + r * 16, 16), 16)]
                g = g.astype(jnp.int32).astype(F32) * scales[s]
                hi = jnp.where(upper, g, 0.0)
                for c, part in ((0, g - hi), (1, hi)):
                    right_part = jnp.where(right, part, 0.0)
                    total[c][1] = total[c][1] + right_part
                    total[c][0] = total[c][0] + (part - right_part)
            for c in range(2):
                acc[c, k, at, 0:128] = total[c][0]
                acc[c, k, at, 128:256] = total[c][1]
        largest = jnp.abs(acc[1 - h, k, 0:8])
        for r in range(1, rows // 8):
            largest = jnp.maximum(largest, jnp.abs(acc[1 - h, k, 8 * r:8 * r + 8]))
        exponent = exponent_of(largest)
        swap_out[k, 0:EXPONENT_ROWS] = exponent_rows([exponent])
        scale = jnp.broadcast_to(jnp.exp2(14.9 - exponent), (16, 2 * ny))

        @pl.loop(0, rows // 16)
        def _(r):
            at = pl.ds(pl.multiple_of(r * 16, 16), 16)
            swap_out[k, pl.ds(pl.multiple_of(EXPONENT_ROWS + r * 16, 16), 16)] = coded(acc[1 - h, k, at] * scale)
        swap(k).start()
        out_ref[k, pl.ds(pl.multiple_of(h * rows, 8), rows)] = acc[h, k]

    def finish(k):
        swap(k).wait()
        exponent = swap_in[k, 0:EXPONENT_ROWS].astype(jnp.int32).astype(F32)[0:1]
        scale = jnp.broadcast_to(jnp.exp2(exponent - 14.9), (16, 2 * ny))

        @pl.loop(0, rows // 16)
        def _(r):
            g = swap_in[k, pl.ds(pl.multiple_of(EXPONENT_ROWS + r * 16, 16), 16)].astype(jnp.int32).astype(F32)
            out_ref[k, pl.ds(pl.multiple_of((1 - h) * rows + r * 16, 8), 16)] = g * scale

    for n in range(8):
        if n < 5:
            forward_y(n)
        if 1 <= n < 6:
            forward_x(n - 1)
        if 2 <= n < 7:
            gather(n - 2)
        if 3 <= n:
            finish(n - 3)

    for k in range(5):
        pl.when(not_self)(lambda: outgoing(0, k).wait_send())
        for i in range(1, shots):
            outgoing(i, k).wait_send()
        for i in range(1, half):
            hop_z(k, i).wait_send()
        for i in range(half):
            stays, moves, go, stay = hop_y(k, i)
            pl.when(moves)(go.wait_send)
        for i in range(8):
            stays, moves, go, stay = hop_x(k, i)
            pl.when(moves)(go.wait_send)


def y_matrix(ny):
    matrix = [[0.0] * (2 * ny) for _ in range(ny)]
    for y in range(ny):
        for k in range(1, 5):
            if y + k < ny:
                matrix[y + k][y] = FIRST[k - 1]
                matrix[y + k][ny + y] = SECOND[k - 1]
            if y - k >= 0:
                matrix[y - k][y] = -FIRST[k - 1]
                matrix[y - k][ny + y] = SECOND[k - 1]
    one = jnp.asarray(matrix, F32).astype(BF16)
    return jnp.concatenate([one, one], axis=0)


def on_device(velocity, epsilon, delta, tilt, azimuth, offsets, sources, traces, adjoint_state, snapshots):
    shots = lax.axis_size("shot")
    slabs = lax.axis_size("slab")
    half = slabs // 2
    _, _, nz, nx, ny = adjoint_state.shape
    nt = snapshots.shape[0]
    depth, width, lanes = velocity.shape
    rows = depth * width // 2
    tiles = nx // 16
    vmem = pl.BlockSpec(memory_space=pltpu.VMEM)
    smem = pl.BlockSpec(memory_space=pltpu.SMEM)
    hbm = pl.BlockSpec(memory_space=pl.ANY)
    dma = pltpu.SemaphoreType.DMA
    params = [m.reshape(depth * width, lanes) for m in (velocity, epsilon, delta, tilt, azimuth)]
    state = adjoint_state.reshape(4, nz, nx, ny)
    frames = snapshots.reshape(nt, 2, nz, nx, ny)
    coded = (8, EXPONENT_ROWS + 5 * rows, ny)
    final, gradients = pl.pallas_call(
        whole_kernel,
        out_shape=(
            jax.ShapeDtypeStruct((2, nz, nx, ny), F32),
            jax.ShapeDtypeStruct((5, 2 * rows, lanes), F32),
        ),
        in_specs=[vmem] * 5 + [smem] * 3 + [hbm, hbm, vmem],
        out_specs=(vmem, vmem),
        scratch_shapes=[
            pltpu.VMEM((2, 5, rows, lanes), BF16),
            pltpu.VMEM((shots, 5, rows, ny), BF16),
            pltpu.VMEM((half, 5, rows, ny), BF16),
            pltpu.VMEM((2, 2, nz + 8, nx + 16, ny), F32),
            pltpu.VMEM((2, nz, nx + 16, ny), F32),
            pltpu.VMEM((2, 2, nz, nx + 16, ny), F32),
            pltpu.VMEM((2, nz, nx, ny), F32),
            pltpu.VMEM((2, 2, nz, nx, ny), F32),
            pltpu.VMEM((tiles, 2 * nz * 16, ny), F32),
            pltpu.VMEM((tiles, 2 * nz * 16, 2 * ny), BF16),
            pltpu.VMEM((tiles, 2 * nz * 16, 2 * ny), BF16),
            pltpu.VMEM((9, nz, nx, ny), F32),
            pltpu.VMEM((8, nz, nx, ny), F32),
            pltpu.VMEM((5, nz, nx, ny), F32),
            pltpu.VMEM((nz, 2 * nx, ny), F32),
            pltpu.VMEM((nt, 2, nz, nx, ny), BF16),
            pltpu.VMEM((5, nx, ny), F32),
            pltpu.VMEM(coded, jnp.int16),
            pltpu.VMEM(coded, jnp.int16),
            pltpu.VMEM(coded, jnp.int16),
            pltpu.VMEM(coded, jnp.int16),
            pltpu.VMEM((2, 5, rows, lanes), F32),
            pltpu.VMEM((5, EXPONENT_ROWS + rows, lanes), jnp.int16),
            pltpu.VMEM((5, EXPONENT_ROWS + rows, lanes), jnp.int16),
            dma((5,)), dma((5,)), dma((5,)), dma((shots, 5)), dma((half, 5)), dma((5,)),
            dma((2, 2, tiles)), dma((2, 2, tiles)),
            dma((3, 5, 8)), dma((3, 5, 8)), dma((5, 5)), dma((5,)), dma((5,)),
        ],
        compiler_params=pltpu.CompilerParams(collective_id=0, has_side_effects=True, vmem_limit_bytes=VMEM_LIMIT),
        name="whole",
    )(*params, offsets.T, sources, traces, state, frames, y_matrix(ny))
    return (gradients.reshape(5, depth, width, lanes), final.reshape(2, 1, nz, nx, ny))


def solution(mesh):
    return jax.shard_map(
        on_device,
        mesh=mesh,
        in_specs=(
            P("shot", "slab", None),
            P("shot", "slab", None),
            P("shot", "slab", None),
            P("shot", "slab", None),
            P("shot", "slab", None),
            P(),
            P("shot"),
            P("shot", None),
            P(None, "shot", "slab", None, None),
            P(None, None, "shot", "slab", None, None),
        ),
        out_specs=(P(None, "shot", "slab", None), P(None, "shot", "slab", None, None)),
        check_vma=False,
    )
```

time: 300 us -> 140 us (0.47)
  the two profiles are of different devices: /device:TPU:17 before, /device:TPU:80 now
where the time goes in v3:
time: 140 us; the launch traced here: 139 us
  Pallas kernels  133 us (95%)
  local copies, waits for them, and re-layouts  4.33 us (3%)
    pallas_call x1, Pallas kernels, on_device(): pl.pallas_call(whole_kernel, out_shape=(jax.ShapeDtypeStruct((2, nz, nx,...  133 us
    unnamed x2, local copies, waits for them, and re-layouts  4.33 us

profile of v3, /device:TPU:80, one launch (start us, length us, event | category | flops | bytes accessed | tf_op | source)
XLA Modules:
  0.0 139.1 jit_solution(6379166442598883960)
XLA Ops:
  1.3 133.4 %whole.1 = (f32[2,12,64,128]{3,2,1,0:T(8,128)}, f32[5,192,256]{2,1,0:T(8,128)}) custom-call(bf16[192,256]{1,0:T(8,128)(2,1)} %bitcast.16, bf16[192,256]{1,0:T(8,128)(2,1)} %bitcast.17, bf16[192,256]{1,0:T(8,128)(2,1)} %bitcast.18, bf16[192,256]{1,0:T(8,128)(2,1)} %bitcast.19, bf16[192,256]{1,0:T(8,128)(2,1)} %bitcast.20, s32[2,8]{1,0:T(2,128)} %bitcast.21, ...), custom_call_target="tpu_custom_call" | custom-call | tf_op jit(solution)/shard_map/whole/pallas_call | solution.py:626
  134.7 2.2 %copy.17 = f32[5,24,8,256]{3,2,1,0:T(8,128)} copy(f32[5,24,8,256]{3,2,1,0:T(8,128)} %bitcast.14) | data formatting | bytes 1966080
  137.0 2.1 %copy.18 = f32[2,1,12,64,128]{4,3,2,1,0:T(8,128)} copy(f32[2,1,12,64,128]{4,3,2,1,0:T(8,128)} %bitcast.15) | data formatting | bytes 1572864

commit v4 on v3

--- a/solution.py
+++ b/solution.py
@@ -16,6 +16,7 @@
 UNIT11 = (4.0 / 105.0) ** 2
 CENTRE = -7175.0 / 64.0
 EXPONENT_ROWS = 16
+CHUNKS = ((0,), (1, 2), (3, 4))
 VMEM_LIMIT = 60 * 1024 * 1024
 
 
@@ -127,7 +128,7 @@
     @pl.loop(0, nz)
     def _(z):
         for f in range(2):
-            for g in (GZ, GY.at[0], GY.at[1]):
+            for g in (GZ, GY):
                 g[f, z, 0:8] = jnp.zeros((8, ny), F32)
                 g[f, z, 8 + nx:16 + nx] = jnp.zeros((8, ny), F32)
 
@@ -158,9 +159,8 @@
         return remote(F.at[slot, :, rows[0], pl.ds(8 + 16 * q, 16)], F.at[slot, :, rows[1], pl.ds(8 + 16 * q, 16)],
                       hsend.at[slot, direction, q], hrecv.at[slot, direction, q], (up, down)[direction])
 
-    def send_halos(slot, q):
-        pl.when(has_up)(lambda: halo(slot, 0, q).start())
-        pl.when(has_down)(lambda: halo(slot, 1, q).start())
+    def send_halos(slot, q, direction):
+        pl.when((has_up, has_down)[direction])(lambda: halo(slot, direction, q).start())
 
     def wait_halos(slot, q):
         @pl.when(has_up)
@@ -207,20 +207,21 @@
     for c in loads[:4]:
         c.wait()
     for q in range(tiles):
-        send_halos(0, q)
+        send_halos(0, q, 0)
+        send_halos(0, q, 1)
 
     def split(value, store):
         hi = value.astype(BF16)
         store(slice(0, ny), hi)
         store(slice(ny, 2 * ny), (value - hi.astype(F32)).astype(BF16))
 
-    def along_y(slot, q):
+    def along_y(q):
         out = jnp.dot(SF[q], y1_ref[...], preferred_element_type=F32)
         for f in range(2):
             for z in range(nz):
                 at = (f * nz + z) * 16
-                GY[slot, f, z, 8 + 16 * q:24 + 16 * q] = out[at:at + 16, 0:ny]
-                YY[slot, f, z, 16 * q:16 * q + 16] = out[at:at + 16, ny:2 * ny]
+                GY[f, z, 8 + 16 * q:24 + 16 * q] = out[at:at + 16, 0:ny]
+                YY[f, z, 16 * q:16 * q + 16] = out[at:at + 16, ny:2 * ny]
 
     for q in range(tiles):
         for f in range(2):
@@ -231,8 +232,6 @@
                 def store(lanes, value):
                     SF[q, at, lanes] = value
                 split(F[0, f, z + 4, 8 + 16 * q:24 + 16 * q], store)
-    for q in range(tiles - 1):
-        along_y(0, q)
 
     ox = lax.rem(offsets_ref[0, me_s], nx)
     oy = lax.rem(offsets_ref[1, me_s], ny)
@@ -313,13 +312,13 @@
         def parts(f):
             def x_of(ref, *lead):
                 return lambda k: ref[(*lead, pl.ds(8 + 16 * q + k, 16))]
-            yy = YY[cur, f, z, at]
+            yy = YY[f, z, at]
             return (
                 ZZ[f, z, at] - yy,
                 second(x_of(F, cur, f, z + 4)) - yy,
                 first(x_of(GZ, f, z)),
                 ZY[q, pl.ds(pl.multiple_of((f * nz + z) * 16, 16), 16)],
-                first(x_of(GY, cur, f, z)),
+                first(x_of(GY, f, z)),
                 yy,
                 F[cur, f, z + 4, inner],
             )
@@ -363,24 +362,24 @@
         cur = lax.rem(t, 2)
         nxt = 1 - cur
         amplitude = traces_ref[0, t]
+        along_y(0)
         wait_halos(cur, 0)
-        along_y(cur, tiles - 1)
         depth_pass(cur, 0)
         for q in range(tiles):
             if q + 1 < tiles:
                 wait_halos(cur, q + 1)
                 depth_pass(cur, q + 1)
+                along_y(q + 1)
             ZY[q] = jnp.dot(SG[q], y1_ref[:, 0:ny], preferred_element_type=F32)
-            if q > 0:
-                along_y(nxt, q - 1)
-
-            @pl.loop(0, 2)
-            def _(zz):
+            for direction in range(2):
                 for z in range(4):
-                    update(t, cur, nxt, q, zz * 8 + z, amplitude)
-            pl.when(t < nt - 1)(lambda: send_halos(nxt, q))
-            for z in range(4, 8):
-                update(t, cur, nxt, q, z, amplitude)
+                    update(t, cur, nxt, q, 8 * direction + z, amplitude)
+                pl.when(t < nt - 1)(lambda: send_halos(nxt, q, direction))
+        for q in range(tiles):
+            @pl.loop(4, 8, step=4)
+            def _(z0):
+                for z in range(4):
+                    update(t, cur, nxt, q, z0 + z, amplitude)
         return carry
 
     lax.fori_loop(0, nt, step, 0)
@@ -441,8 +440,9 @@
             MX[k, 8 * j:8 * j + 8] = jnp.broadcast_to(jnp.exp2(14.9 - exponents[k]), (8, ny))
         GQ[j, 0:EXPONENT_ROWS] = exponent_rows(exponents)
 
-    def chunk(k):
-        return pl.ds(0, EXPONENT_ROWS + rows) if k == 0 else pl.ds(EXPONENT_ROWS + k * rows, rows)
+    def chunk(n):
+        begin = EXPONENT_ROWS + CHUNKS[n][0] * rows if n else 0
+        return pl.ds(begin, EXPONENT_ROWS + (CHUNKS[n][-1] + 1) * rows - begin)
 
     def hop_z(k, i):
         j = lax.rem(j_me + i, half)
@@ -452,17 +452,18 @@
     def own_z(k):
         return pltpu.make_async_copy(GQ.at[j_me, chunk(k)], first_in.at[j_me, chunk(k)], rloc.at[k, 0])
 
-    for k in range(5):
-        @pl.loop(0, nz // 2)
-        def _(zz):
-            for j in range(half):
-                scale = MX[k, 8 * j:8 * j + 8]
-                pair = jnp.concatenate([TRIG[k, 2 * zz, 8 * j:8 * j + 8] * scale,
-                                        TRIG[k, 2 * zz + 1, 8 * j:8 * j + 8] * scale], axis=0)
-                GQ[j, pl.ds(pl.multiple_of(EXPONENT_ROWS + k * rows + zz * 16, 16), 16)] = coded(pair)
-        own_z(k).start()
+    for n, members in enumerate(CHUNKS):
+        for k in members:
+            @pl.loop(0, nz // 2)
+            def _(zz):
+                for j in range(half):
+                    scale = MX[k, 8 * j:8 * j + 8]
+                    pair = jnp.concatenate([TRIG[k, 2 * zz, 8 * j:8 * j + 8] * scale,
+                                            TRIG[k, 2 * zz + 1, 8 * j:8 * j + 8] * scale], axis=0)
+                    GQ[j, pl.ds(pl.multiple_of(EXPONENT_ROWS + k * rows + zz * 16, 16), 16)] = coded(pair)
+        own_z(n).start()
         for i in range(1, half):
-            hop_z(k, i).start()
+            hop_z(n, i).start()
 
     def hop_y(k, i):
         j = lax.rem(j_me + i, half)
@@ -512,7 +513,7 @@
     def swap(k):
         return remote(swap_out.at[k], swap_in.at[k], ssend.at[k], srecv.at[k], partner)
 
-    def gather(k):
+    def arrive(k):
         for i in range(shots):
             s = lax.rem(me_s + i, shots)
             here = s // 2 == x
@@ -522,6 +523,8 @@
             pl.when(away)(lambda: remote(
                 second_in.at[0, chunk(k)], third_in.at[s, chunk(k)], rsend.at[2, k, 0], rrecv.at[2, k, s],
                 (s // 2 * 2 + y_hi, me_b)).wait_recv())
+
+    def gather(k):
         scales = []
         for s in range(shots):
             exponents = third_in[s, 0:EXPONENT_ROWS].astype(jnp.int32).astype(F32)
@@ -568,27 +571,30 @@
             g = swap_in[k, pl.ds(pl.multiple_of(EXPONENT_ROWS + r * 16, 16), 16)].astype(jnp.int32).astype(F32)
             out_ref[k, pl.ds(pl.multiple_of((1 - h) * rows + r * 16, 8), 16)] = g * scale
 
-    for n in range(8):
-        if n < 5:
+    for n in range(len(CHUNKS) + 2):
+        if n < len(CHUNKS):
             forward_y(n)
-        if 1 <= n < 6:
+        if 1 <= n < len(CHUNKS) + 1:
             forward_x(n - 1)
-        if 2 <= n < 7:
-            gather(n - 2)
-        if 3 <= n:
-            finish(n - 3)
+        if 2 <= n:
+            arrive(n - 2)
+            for k in CHUNKS[n - 2]:
+                gather(k)
+    for k in range(5):
+        finish(k)
 
     for k in range(5):
         pl.when(not_self)(lambda: outgoing(0, k).wait_send())
         for i in range(1, shots):
             outgoing(i, k).wait_send()
+    for n in range(len(CHUNKS)):
         for i in range(1, half):
-            hop_z(k, i).wait_send()
+            hop_z(n, i).wait_send()
         for i in range(half):
-            stays, moves, go, stay = hop_y(k, i)
+            stays, moves, go, stay = hop_y(n, i)
             pl.when(moves)(go.wait_send)
         for i in range(8):
-            stays, moves, go, stay = hop_x(k, i)
+            stays, moves, go, stay = hop_x(n, i)
             pl.when(moves)(go.wait_send)
 
 
@@ -637,9 +643,9 @@
             pltpu.VMEM((half, 5, rows, ny), BF16),
             pltpu.VMEM((2, 2, nz + 8, nx + 16, ny), F32),
             pltpu.VMEM((2, nz, nx + 16, ny), F32),
-            pltpu.VMEM((2, 2, nz, nx + 16, ny), F32),
+            pltpu.VMEM((2, nz, nx + 16, ny), F32),
             pltpu.VMEM((2, nz, nx, ny), F32),
-            pltpu.VMEM((2, 2, nz, nx, ny), F32),
+            pltpu.VMEM((2, nz, nx, ny), F32),
             pltpu.VMEM((tiles, 2 * nz * 16, ny), F32),
             pltpu.VMEM((tiles, 2 * nz * 16, 2 * ny), BF16),
             pltpu.VMEM((tiles, 2 * nz * 16, 2 * ny), BF16),

time: 140 us -> 135 us (0.964)
  Pallas kernels: 133 us -> 130 us
    pallas_call x1, Pallas kernels: 133 us -> 130 us  [on_device(): pl.pallas_call(whole_kernel, out_shape=(jax.ShapeDtypeStruct((2, nz, nx,...]
where the time goes in v4:
time: 135 us
  Pallas kernels  130 us (96%)
  local copies, waits for them, and re-layouts  4.33 us (3%)
    pallas_call x1, Pallas kernels, on_device(): pl.pallas_call(whole_kernel, out_shape=(jax.ShapeDtypeStruct((2, nz, nx,...  130 us
    unnamed x2, local copies, waits for them, and re-layouts  4.33 us

profile of v4, /device:TPU:80, one launch (start us, length us, event | category | flops | bytes accessed | tf_op | source)
XLA Modules:
  0.0 135.1 jit_solution(11911770722670583444)
XLA Ops:
  1.3 129.5 %whole.1 = (f32[2,12,64,128]{3,2,1,0:T(8,128)}, f32[5,192,256]{2,1,0:T(8,128)}) custom-call(bf16[192,256]{1,0:T(8,128)(2,1)} %bitcast.16, bf16[192,256]{1,0:T(8,128)(2,1)} %bitcast.17, bf16[192,256]{1,0:T(8,128)(2,1)} %bitcast.18, bf16[192,256]{1,0:T(8,128)(2,1)} %bitcast.19, bf16[192,256]{1,0:T(8,128)(2,1)} %bitcast.20, s32[2,8]{1,0:T(2,128)} %bitcast.21, ...), custom_call_target="tpu_custom_call" | custom-call | tf_op jit(solution)/shard_map/whole/pallas_call | solution.py:632
  130.8 2.2 %copy.17 = f32[5,24,8,256]{3,2,1,0:T(8,128)} copy(f32[5,24,8,256]{3,2,1,0:T(8,128)} %bitcast.14) | data formatting | bytes 1966080
  133.1 2.1 %copy.18 = f32[2,1,12,64,128]{4,3,2,1,0:T(8,128)} copy(f32[2,1,12,64,128]{4,3,2,1,0:T(8,128)} %bitcast.15) | data formatting | bytes 1572864

commit v5 on v4

--- a/solution.py
+++ b/solution.py
@@ -362,14 +362,14 @@
         cur = lax.rem(t, 2)
         nxt = 1 - cur
         amplitude = traces_ref[0, t]
-        along_y(0)
+        for q in range(tiles):
+            along_y(q)
         wait_halos(cur, 0)
         depth_pass(cur, 0)
         for q in range(tiles):
             if q + 1 < tiles:
                 wait_halos(cur, q + 1)
                 depth_pass(cur, q + 1)
-                along_y(q + 1)
             ZY[q] = jnp.dot(SG[q], y1_ref[:, 0:ny], preferred_element_type=F32)
             for direction in range(2):
                 for z in range(4):
@@ -596,6 +596,11 @@
         for i in range(8):
             stays, moves, go, stay = hop_x(n, i)
             pl.when(moves)(go.wait_send)
+
+
+def place_kernel(gradients_ref, final_ref, gradients_out, final_out):
+    gradients_out[...] = gradients_ref[...]
+    final_out[...] = final_ref[...]
 
 
 def y_matrix(ny):
@@ -669,6 +674,18 @@
         compiler_params=pltpu.CompilerParams(collective_id=0, has_side_effects=True, vmem_limit_bytes=VMEM_LIMIT),
         name="whole",
     )(*params, offsets.T, sources, traces, state, frames, y_matrix(ny))
+    gradients, final = pl.pallas_call(
+        place_kernel,
+        out_shape=(
+            jax.ShapeDtypeStruct((5, 2 * rows, lanes), F32),
+            jax.ShapeDtypeStruct((2, nz, nx, ny), F32),
+        ),
+        grid=(2,),
+        in_specs=[pl.BlockSpec((5, rows, lanes), lambda i: (0, i, 0)), pl.BlockSpec((1, nz, nx, ny), lambda i: (i, 0, 0, 0))],
+        out_specs=(pl.BlockSpec((5, rows, lanes), lambda i: (0, i, 0)), pl.BlockSpec((1, nz, nx, ny), lambda i: (i, 0, 0, 0))),
+        compiler_params=pltpu.CompilerParams(vmem_limit_bytes=VMEM_LIMIT),
+        name="place",
+    )(gradients, final)
     return (gradients.reshape(5, depth, width, lanes), final.reshape(2, 1, nz, nx, ny))
 
 

time: 135 us -> 133 us (0.985)
  local copies, waits for them, and re-layouts: 4.33 us -> 0 us
  Pallas kernels: 130 us -> 132 us
    unnamed x2 -> x0, local copies, waits for them, and re-layouts: 4.33 us -> none
    pallas_call x0 -> x1, Pallas kernels: none -> 2.42 us  [on_device(): pl.pallas_call(place_kernel, out_shape=(jax.ShapeDtypeStruct((5, 2 * rows...]
where the time goes in v5:
time: 133 us
  Pallas kernels  132 us (99%)
    pallas_call x1, Pallas kernels, on_device(): pl.pallas_call(whole_kernel, out_shape=(jax.ShapeDtypeStruct((2, nz, nx,...  129 us

profile of v5, /device:TPU:80, one launch (start us, length us, event | category | flops | bytes accessed | tf_op | source)
XLA Modules:
  0.0 132.9 jit_solution(7623796944343375682)
XLA Ops:
  1.3 129.2 %whole.1 = (f32[2,12,64,128]{3,2,1,0:T(8,128)}, f32[5,192,256]{2,1,0:T(8,128)}) custom-call(bf16[192,256]{1,0:T(8,128)(2,1)} %bitcast.14, bf16[192,256]{1,0:T(8,128)(2,1)} %bitcast.15, bf16[192,256]{1,0:T(8,128)(2,1)} %bitcast.16, bf16[192,256]{1,0:T(8,128)(2,1)} %bitcast.17, bf16[192,256]{1,0:T(8,128)(2,1)} %bitcast.18, s32[2,8]{1,0:T(2,128)} %bitcast.19, ...), custom_call_target="tpu_custom_call" | custom-call | tf_op jit(solution)/shard_map/whole/pallas_call | solution.py:637
  130.5 2.4 %place.1 = (f32[5,192,256]{2,1,0:T(8,128)}, f32[2,12,64,128]{3,2,1,0:T(8,128)}) custom-call(f32[5,192,256]{2,1,0:T(8,128)} %get-tuple-element.6.gradients_ref, f32[2,12,64,128]{3,2,1,0:T(8,128)} %get-tuple-element.7.final_ref), custom_call_target="tpu_custom_call" | custom-call | tf_op jit(solution)/shard_map/place/pallas_call | solution.py:677
